TPU v7x, 32 devices: a whole 2x2x4 slice. The times are simulated.
32 devices in a mesh: grp: 2 (over y), gz: 8 (over z, x), gy: 2 (over core).
Axes of the slice: x: 2, y: 2, z: 4, core: 2. Of those that a mesh axis runs over, the one named last changes fastest.
Arguments:
- estimate_start: float32 [256, 64, 256], P(('grp', 'gz'), 'gy'), parts along dimension 0, may hold values from 0.5 to 2
- view_images: float32 [4, 256, 64, 256], P(None, ('grp', 'gz'), 'gy'), parts along dimension 1, may hold values from 0.5 to 2
- psf_taps: float32 [4, 3, 31], replicated, may hold values from 0.1 to 1
Outputs:
- estimate: float32 [256, 64, 256], P(('grp', 'gz'), 'gy'), parts along dimension 0
There are 2 independent parts, one for each index of `grp`. A program takes and returns all parts, laid end to end along the dimension named above; an argument that names none is the same for every part. Nothing has to cross between parts.
All inputs are finite; a program needn't handle non-finite values.
Results may differ from a plain program's by a relative error of at most 0.00022.
Values sent between devices are 32-bit elements; how exact they have to be, the bound alone decides.
No kernel may reach another device: no remote copies, remote signals or barrier semaphores. Data moves between devices by JAX's collectives and lax.ppermute only.
A program may use at most 64 MiB of HBM per device.

v0:
```python
import functools

import jax
import jax.numpy as jnp
from jax import lax
from jax.experimental import pallas as pl
from jax.experimental.pallas import tpu as pltpu
from jax.sharding import PartitionSpec as P

ITERS = 2
AXES = ("gz", "gy")
EDGE = 32
F32, BF16 = jnp.float32, jnp.bfloat16


def spot(zp, xp, c):
    return (2 * zp + xp) * 2 + c


def core_swap(n):
    return [(spot(z, x, c), spot(z, x, 1 - c)) for z in range(n) for x in range(2) for c in range(2)]


def half_swap(n):
    return [(spot(z, x, c), spot(z, 1 - x, c)) for z in range(n) for x in range(2) for c in range(2)]


def chip_swap(n):
    pairs = []
    for x in range(2):
        for z in range(n - 1):
            pairs += [(spot(z, x, 1), spot(z + 1, x, 0)), (spot(z + 1, x, 0), spot(z, x, 1))]
        pairs += [(spot(0, x, 0), spot(0, 1 - x, 0)), (spot(n - 1, x, 1), spot(n - 1, 1 - x, 1))]
    return pairs


def entry_one(n):
    pairs = []
    for z in range(n):
        pairs += [
            (spot(z, 0, 1), spot(z, 0, 0)),
            (spot(z, 0, 0), spot(z, 1, 0)),
            (spot(z, 1, 0), spot(z, 1, 1)),
            (spot(z, 1, 1), spot(z, 0, 1)),
        ]
    return pairs


def entry_two(n, over_z):
    pairs = []
    for z in range(n):
        pairs += [(spot(z, 0, 1), spot(z, 1, 0)), (spot(z, 1, 0), spot(z, 0, 1))]
        if over_z and n % 2 == 0:
            pairs += [(spot(z, 0, 0), spot(z ^ 1, 0, 0)), (spot(z, 1, 1), spot(z ^ 1, 1, 1))]
        else:
            pairs += [(spot(z, 0, 0), spot(z, 1, 1)), (spot(z, 1, 1), spot(z, 0, 0))]
    return pairs


def back(pairs):
    return [(target, source) for source, target in pairs]


def toeplitz(row, half):
    size = row.shape[1]
    base = pltpu.roll(jnp.broadcast_to(row, (size, size)), size - half, 1)
    return pltpu.roll(base, 0, 1, stride=1, stride_axis=0)


def taps_row(taps_ref, view, axis, row_ref):
    taps = taps_ref.shape[2]
    row_ref[...] = jnp.zeros(row_ref.shape, F32)
    row_ref[:, :taps] = taps_ref[view, axis : axis + 1, :]
    row = row_ref[...]
    return row / jnp.sum(row, axis=1, keepdims=True)


def put_halves(ref, matrix):
    ref[0], ref[1] = split(matrix)


def lanes(shape, axis):
    return lax.broadcasted_iota(jnp.int32, shape, axis)


def split(value):
    high = value.astype(BF16)
    return high, (value - high.astype(F32)).astype(BF16)


def dot(a, b):
    return jnp.dot(a, b, preferred_element_type=F32)


def times_right(value, mat_ref):
    high, low = split(value)
    return dot(high, mat_ref[0]) + (dot(low, mat_ref[0]) + dot(high, mat_ref[1]))


def times_left(mat_ref, value):
    high, low = split(value)
    return dot(mat_ref[0], high) + (dot(mat_ref[0], low) + dot(mat_ref[1], high))


def call(kernel, outs, *args, scratch=(), cost=0):
    def spec(a):
        small = a.ndim == 1
        return pl.BlockSpec(memory_space=pltpu.SMEM if small else pltpu.VMEM)

    return pl.pallas_call(
        kernel,
        out_shape=[jax.ShapeDtypeStruct(s, F32) if isinstance(s, tuple) else s for s in outs],
        in_specs=[spec(a) for a in args],
        out_specs=[pl.BlockSpec(memory_space=pltpu.VMEM) for _ in outs],
        scratch_shapes=list(scratch),
        compiler_params=pltpu.CompilerParams(vmem_limit_bytes=24 * 1024 * 1024),
        cost_estimate=pl.CostEstimate(flops=1 + cost * 10**9, bytes_accessed=1 + cost * 3 * 10**6, transcendentals=0),
    )(*args)


def place():
    core, gz, n = lax.axis_index("gy"), lax.axis_index("gz"), lax.axis_size("gz") // 2
    at_end = ((gz < 2) & (core == 0)) | ((gz >= 2 * n - 2) & (core == 1))
    return core, gz % 2, jnp.where(at_end, 0, 1)


def cut_kernel(est_ref, one_ref, two_ref):
    planes, rows, cols = est_ref.shape
    wide = cols // 2
    groups = wide // EDGE
    each = planes // groups
    lower = place()[0] == 0
    packed = None
    for g in range(groups):
        at = slice(each * g, each * (g + 1))
        block = est_ref[at].reshape(each * rows, cols)
        low, high = block[:, :wide].reshape(each, rows, wide), block[:, wide:].reshape(each, rows, wide)
        one_ref[at] = jnp.where(lower, high, low)
        two_ref[at] = jnp.where(lower, low, high)
        turned = pltpu.roll(block, (EDGE * g - wide + EDGE // 2) % cols, 1)[:, :wide]
        packed = turned if packed is None else jnp.where(lanes(turned.shape, 1) // EDGE == g, turned, packed)
    packed = packed.reshape(each, rows, wide)
    one_ref[planes:] = packed
    two_ref[planes:] = packed


def first_kernel(
    one_ref, two_ref, kept_ref, mat_x, mat_around, mat_y,
    main_out, window_out, part_out, core_low_ref, core_high_ref, low_ref, high_ref,
):
    planes, rows, cols = main_out.shape
    half = rows // 2
    first = place()[1] == 0

    one, two = one_ref[...], jnp.where(stays(), kept_ref[...], two_ref[...])
    low, high = jnp.where(first, two, one), jnp.where(first, one, two)
    main_out[:, :half], main_out[:, half:] = low[:planes], high[:planes]
    groups = cols // EDGE
    each = planes // groups
    size = each * rows
    window = jnp.concatenate([low[planes:], high[planes:]], axis=1).reshape(size, cols)
    window_out[...] = window
    for pair in range(groups // 2):
        both = (2 * pair, 2 * pair + 1)
        blocks = [main_out[each * g : each * (g + 1)].reshape(size, cols) for g in both]
        part = jnp.concatenate([times_right(block, mat_x) for block in blocks], axis=1)
        part = times_left(mat_y, part + times_right(window, mat_around.at[pair]))
        for side, g in enumerate(both):
            put_rows(
                part_out, slice(each * g, each * (g + 1)),
                part[:, cols * side : cols * (side + 1)].reshape(each, rows, cols),
            )
    put_sent(part_out, (core_low_ref, core_high_ref), low_ref, high_ref)


def stays():
    core, xp, _ = place()
    return core == xp


def put_rows(out_ref, at, block):
    rows = out_ref.shape[2]
    out_ref[0, at], out_ref[1, at] = block[:, :rows], block[:, rows:]


def put_sent(out_ref, core_ref, low_ref, high_ref):
    flags = place()
    sent = low_ref.shape[0]
    spare = out_ref.shape[1] - sent
    at = pl.ds((1 - flags[0]) * spare, sent)
    core_ref[0][...], core_ref[1][...] = out_ref[0, at], out_ref[1, at]
    at = pl.ds(flags[0] * spare, sent)
    low_ref[...], high_ref[...] = out_ref[0, at], out_ref[1, at]


def pack_edge(blocks):
    first = jnp.where(place()[1] == 0, EDGE, 0)
    packed = None
    for g, block in enumerate(blocks):
        cols = block.shape[1]
        turned = pltpu.roll(block, (EDGE * g + first) % cols, 1)
        if packed is None:
            packed = turned
        else:
            lane = lax.broadcasted_iota(jnp.int32, block.shape, 1)
            packed = jnp.where(lane // EDGE == g, turned, packed)
    return packed


def mats_kernel(
    taps_ref, back_x_ref, back_window_ref, x_ref, window_ref, y_ref, ya_ref, z_ref,
    full, turned, row_ref, *, view, rows
):
    size, wide = full.shape[0], x_ref.shape[1]
    taps = z_ref.shape[0]
    groups = wide // EDGE
    near = EDGE // 2
    flags = place()
    first = flags[1] == 0
    diff = lanes((size, size), 0) - lanes((size, size), 1)
    band_x = jnp.where(jnp.abs(diff) <= taps // 2, toeplitz(taps_row(taps_ref, view, 2, row_ref), taps // 2), 0.0)
    full[...] = band_x
    turned[...] = band_x.T
    main = pl.ds(pl.multiple_of(flags[1] * wide, wide), wide)
    here = full[main, :]
    block = jnp.where(first, here[:, :wide], here[:, wide:])
    lane = lanes((wide, wide), 1)
    for g in range(groups):
        moved = pltpu.roll(here, (EDGE * g - wide + near) % size, 1)[:, :wide]
        moved = jnp.where(lane // EDGE == g, moved, 0.0)
        put_halves(back_x_ref.at[g], jnp.concatenate([block, moved], axis=1))
    beyond = full[pl.ds(pl.multiple_of(jnp.where(first, wide, wide - EDGE), EDGE), EDGE), :]
    parts = []
    for g in range(groups):
        moved = pltpu.roll(beyond, (EDGE * g - wide + near) % size, 1)[:, :wide]
        parts.append(jnp.where(lanes((EDGE, wide), 1) // EDGE == g, moved, 0.0))
    put_halves(back_window_ref, jnp.concatenate(parts, axis=0))
    here = turned[main, :]
    block = jnp.where(first, here[:, :wide], here[:, wide:])
    row = lanes((wide, wide), 0)
    apart = jnp.where(first, row, row - near)
    put_halves(x_ref, jnp.where((apart >= 0) & (apart < wide - near), block, 0.0))
    around = turned[wide - near : wide + near, :]
    around = jnp.where(first, around[:, :wide], around[:, wide:])
    zero = jnp.zeros((EDGE, wide), F32)
    for pair in range(groups // 2):
        both = [
            jnp.concatenate([around if g == 2 * pair + side else zero for g in range(groups)], axis=0)
            for side in range(2)
        ]
        put_halves(window_ref.at[pair], jnp.concatenate(both, axis=1))
    band_y = toeplitz(taps_row(taps_ref, view, 1, row_ref), taps // 2)
    band_y = jnp.where(lanes((size, size), 0) // rows == lanes((size, size), 1) // rows, band_y, 0.0)
    put_halves(y_ref, band_y)
    put_halves(ya_ref, band_y.T)
    line = taps_row(taps_ref, view, 0, row_ref)
    for tap in range(taps):
        z_ref[tap] = jnp.broadcast_to(line[:, tap : tap + 1], z_ref.shape[1:])


def add_planes(total, taps_ref, field, flip):
    taps = taps_ref.shape[0]
    half = taps // 2
    for tap in range(taps):
        weight = None
        for i in range(len(total)):
            plane = field.get(i + tap - half)
            if plane is None:
                continue
            if weight is None:
                weight = taps_ref[taps - 1 - tap if flip else tap]
            term = weight * plane
            total[i] = term if total[i] is None else total[i] + term
    return total


def own_z_kernel(taps, own_ref, core_ref, out_ref, *, flip):
    parts, planes, rows, _ = own_ref.shape
    flags = place()
    half = taps.shape[0] // 2
    tiles = rows // 8
    for core in range(2):

        @pl.when(flags[0] == core)
        def _():
            def step(i, carry):
                part, at = i // tiles, pl.ds(pl.multiple_of(i % tiles * 8, 8), 8)
                field = {j: own_ref[part, j, at, :] for j in range(planes)}
                for j in range(half):
                    field[planes + j if core == 0 else j - half] = core_ref[part, j, at, :]
                total = add_planes([None] * planes, taps, field, flip)
                for j in range(planes):
                    out_ref[part, j, at, :] = total[j]
                return carry

            lax.fori_loop(0, parts * tiles, step, 0)


def own_z_half_kernel(taps, own_ref, core_ref, out_ref):
    grown = (1, *own_ref.shape)
    own_z_kernel(taps, own_ref.reshape(grown), core_ref.reshape(1, *core_ref.shape), out_ref.reshape(grown), flip=True)


def own_z_first_kernel(taps, own_ref, core_low_ref, core_high_ref, out_ref, core_ref):
    core_ref[0], core_ref[1] = core_low_ref[...], core_high_ref[...]
    own_z_kernel(taps, own_ref, core_ref, out_ref, flip=False)


def finish_z(taps, part_ref, chip_ref, flip, put):
    planes, rows, _ = part_ref.shape
    half = chip_ref.shape[0]
    flags = place()
    for case in range(3):
        wanted = (flags[2] == 0) if case == 2 else (flags[2] == 1) & (flags[0] == case)

        @pl.when(wanted)
        def _():
            def step(i, carry):
                at = pl.ds(pl.multiple_of(i * 8, 8), 8)
                total = [part_ref[j, at, :] for j in range(planes)]
                if case < 2:
                    first = -half if case == 0 else planes
                    field = {first + j: chip_ref[j, at, :] for j in range(half)}
                    total = add_planes(total, taps, field, flip)
                put(at, total)
                return carry

            lax.fori_loop(0, rows // 8, step, 0)


def ratio_kernel(taps, part_ref, chip_ref, one_ref, two_ref, kept_ref, out_ref, core_ref, send_ref, *, side):
    planes = part_ref.shape[1]
    flags = place()
    from_two, keep = flags[1] == side, stays()

    def put(at, blurred):
        for j in range(planes):
            two = jnp.where(keep, kept_ref[j, at, :], two_ref[j, at, :])
            out_ref[j, at, :] = jnp.where(from_two, two, one_ref[j, at, :]) / blurred[j]

    finish_z(taps, part_ref.at[side], chip_ref, False, put)
    sent = send_ref.shape[0]
    core_ref[...] = out_ref[pl.ds((1 - flags[0]) * (planes - sent), sent)]
    send_ref[...] = out_ref[pl.ds(flags[0] * (planes - sent), sent)]


def back_kernel(taps, part_ref, chip_ref, out_ref):
    def put(at, total):
        for j in range(len(total)):
            out_ref[j, at, :] = total[j]

    finish_z(taps, part_ref, chip_ref, True, put)


def joined_rows(low_ref, high_ref, at):
    block = jnp.concatenate([low_ref[at], high_ref[at]], axis=1)
    return block.reshape(block.shape[0] * block.shape[1], block.shape[2])


def back_edge_kernel(taps, part_ref, chip_ref, out_ref, edge_ref):
    back_kernel(taps, part_ref, chip_ref, out_ref)
    planes, rows, cols = out_ref.shape
    groups = cols // EDGE
    each = planes // groups
    packed = pack_edge([out_ref[each * g : each * (g + 1)].reshape(each * rows, cols) for g in range(groups)])
    edge_ref[...] = packed.reshape(edge_ref.shape)


def far_kernel(low_ref, high_ref, est_ref, mat_ya, mat_xa, mat_x, mat_y, est_out, corr_out, part_out):
    planes, rows, cols = est_ref.shape
    groups = cols // EDGE
    each = planes // groups
    size = each * rows
    corr_out[...] = jnp.zeros(corr_out.shape, F32)

    def step(pair, carry):
        both = [(2 * pair + side, pl.ds(each * (2 * pair + side), each)) for side in range(2)]
        block = jnp.concatenate([joined_rows(low_ref, high_ref, at) for _, at in both], axis=1)
        block = times_left(mat_ya, block)
        wide = []
        for side, (g, at) in enumerate(both):
            corr = times_right(block[:, cols * side : cols * (side + 1)], mat_xa.at[g])
            corr_out[...] += corr[:, cols:]
            est = est_ref[at].reshape(size, cols) * corr[:, :cols]
            est_out[at] = est.reshape(each, rows, cols)
            if part_out is not None:
                wide.append(times_right(est, mat_x))
        if part_out is not None:
            part = times_left(mat_y, jnp.concatenate(wide, axis=1))
            for side, (_, at) in enumerate(both):
                part_out[at] = part[:, cols * side : cols * (side + 1)].reshape(each, rows, cols)
        return carry

    lax.fori_loop(0, groups // 2, step, 0)


def far_last_kernel(low_ref, high_ref, est_ref, mat_ya, mat_xa, one_out, two_out, corr_out, est):
    far_kernel(low_ref, high_ref, est_ref, mat_ya, mat_xa, None, None, est, corr_out, None)
    half = est.shape[1] // 2
    first = place()[1] == 0
    low, high = est[:, :half], est[:, half:]
    one_out[...] = jnp.where(first, high, low)
    two_out[...] = jnp.where(first, low, high)


def near_window(edge_low, edge_high, corr_ref, window_ref, mat_ya, mat_window):
    edge = times_left(mat_ya, joined_rows(edge_low, edge_high, slice(None)))
    return window_ref[...] * (corr_ref[...] + times_right(edge, mat_window))


def near_kernel(
    edge_low, edge_high, corr_ref, window_ref, part_ref, mat_ya, mat_window, mat_y, mat_around,
    window_out, part_out, core_ref, low_ref, high_ref,
):
    planes, rows, cols = part_ref.shape
    groups = cols // EDGE
    each = planes // groups
    window = near_window(edge_low, edge_high, corr_ref, window_ref, mat_ya, mat_window)
    window_out[...] = window
    blurred = times_left(mat_y, window)

    def step(pair, carry):
        share = times_right(blurred, mat_around.at[pair])
        for side in range(2):
            at = pl.ds(each * (2 * pair + side), each)
            put_rows(
                part_out, at, part_ref[at] + share[:, cols * side : cols * (side + 1)].reshape(each, rows, cols)
            )
        return carry

    lax.fori_loop(0, groups // 2, step, 0)
    put_sent(part_out, (core_ref.at[0], core_ref.at[1]), low_ref, high_ref)


def near_last_kernel(edge_low, edge_high, corr_ref, window_ref, mat_ya, mat_window, out_ref):
    window = near_window(edge_low, edge_high, corr_ref, window_ref, mat_ya, mat_window)
    each, half, cols = out_ref.shape
    window = window.reshape(each, 2 * half, cols)
    out_ref[...] = jnp.where(place()[1] == 0, window[:, :half], window[:, half:])


def leave_kernel(one_ref, two_ref, kept_ref, window_ref, window_kept_ref, out_ref):
    planes, rows, wide = one_ref.shape
    groups = wide // EDGE
    each = planes // groups
    lower = place()[0] == 0
    one, two = one_ref[...], jnp.where(stays(), kept_ref[...], two_ref[...])
    window = jnp.where(stays(), window_kept_ref[...], window_ref[...]).reshape(each * rows, wide)
    window = jnp.concatenate([window, window], axis=1)
    from_cut = lanes(window.shape, 1) - wide + EDGE // 2
    for g in range(groups):
        at = slice(each * g, each * (g + 1))
        block = jnp.concatenate([jnp.where(lower, two[at], one[at]), jnp.where(lower, one[at], two[at])], axis=2)
        turned = pltpu.roll(window, (wide - EDGE // 2 - EDGE * g) % (2 * wide), 1)
        block = jnp.where((from_cut >= 0) & (from_cut < EDGE), turned, block.reshape(each * rows, 2 * wide))
        out_ref[at] = block.reshape(each, rows, 2 * wide)


def local(estimate_start, view_images, psf_taps):
    planes, rows_dev, cols = estimate_start.shape
    views, _, taps = psf_taps.shape
    half = taps // 2
    n = lax.axis_size("gz") // 2
    rows, wide = rows_dev * lax.axis_size("gy"), cols // 2
    core = lax.axis_index("gy")
    send = lambda value, pairs: lax.ppermute(value, AXES, pairs)
    groups = wide // EDGE
    rows_y = planes * rows // groups
    field, packed, piece = (planes, rows, wide), (rows_y, wide), (planes, rows_dev, wide)
    sent, by_half = (half, rows_dev, wide), (2, *piece)
    sent_both, edge = (2, *sent), (planes // groups, rows_dev, wide)

    def mats(view):
        pair = lambda *shape: jax.ShapeDtypeStruct(shape, BF16)
        return call(
            functools.partial(mats_kernel, view=view, rows=rows),
            [
                pair(groups, 2, wide, 2 * wide),
                pair(2, wide, wide),
                pair(2, wide, wide),
                pair(groups // 2, 2, wide, 2 * wide),
                pair(2, rows_y, rows_y),
                pair(2, rows_y, rows_y),
                (taps, 8, wide),
            ],
            psf_taps, scratch=[pltpu.VMEM((cols, cols), F32)] * 2 + [pltpu.VMEM((1, cols), F32)],
        )

    def pieces(value, *index):
        def cut(half):
            start = (*index, 0, 0, wide * half)
            return lax.dynamic_slice(value, start, (1,) * len(index) + piece).reshape(piece)

        return cut(1 - core), cut(core)

    entry = (planes + planes // groups, rows_dev, wide)
    one, kept = call(cut_kernel, [entry, entry], estimate_start)
    one, two = send(one, entry_one(n)), send(kept, entry_two(n, True))
    back_x, back_window, mat_x, around, mat_y, mat_ya, k_z = mats(0)
    image = pieces(view_images, 0)
    image = send(image[0], entry_one(n)), send(image[1], entry_two(n, False)), image[1]
    main, window, part, core_low, core_high, *sent_planes = call(
        first_kernel, [field, packed, by_half, sent, sent, sent, sent], one, two, kept, mat_x, around, mat_y
    )

    for view in range(views):
        for step in range(ITERS):
            last = step + 1 == ITERS
            ahead = view + 1 < views
            if ahead and not last:
                images, _ = lax.optimization_barrier((view_images, part))
                next_pieces = pieces(images, view + 1)
            if view == 0 and step == 0:
                (own,) = call(
                    own_z_first_kernel, [by_half], k_z, part,
                    send(core_low, core_swap(n)), send(core_high, core_swap(n)), scratch=[pltpu.VMEM(sent_both, F32)],
                )
            else:
                (own,) = call(
                    functools.partial(own_z_kernel, flip=False), [by_half], k_z, part, send(sent_core, core_swap(n))
                )
            chip = [send(s, chip_swap(n)) for s in sent_planes]
            if view + 1 < views and not last:
                chip[1], *next_mats = lax.optimization_barrier((chip[1], *mats(view + 1)))
            ratio, sent_core, sent_low = call(
                functools.partial(ratio_kernel, side=0), [piece, sent, sent], k_z, own, chip[0], *image
            )
            core_low, chip_low = send(sent_core, core_swap(n)), send(sent_low, chip_swap(n))
            chip_high, _ = lax.optimization_barrier((chip[1], ratio))
            (low,) = call(own_z_half_kernel, [piece], k_z, ratio, core_low)
            ratio, sent_core, sent_high = call(
                functools.partial(ratio_kernel, side=1), [piece, sent, sent], k_z, own, chip_high, *image
            )
            core_high, chip_high = send(sent_core, core_swap(n)), send(sent_high, chip_swap(n))
            low, edge_low = call(back_edge_kernel, [piece, edge], k_z, low, chip_low, cost=10)
            edge_low = send(edge_low, half_swap(n))
            core_high, _ = lax.optimization_barrier((core_high, low))
            (high,) = call(own_z_half_kernel, [piece], k_z, ratio, core_high)
            if ahead:
                if last:
                    next_kept, _ = lax.optimization_barrier((next_kept, low))
                    next_two = send(next_kept, entry_two(n, True))
                else:
                    next_one, next_kept, _ = lax.optimization_barrier((*next_pieces, low))
                    next_one = send(next_one, entry_one(n))
            high, edge_high = call(back_edge_kernel, [piece, edge], k_z, high, chip_high)
            edge_high = send(edge_high, half_swap(n))
            if not ahead:
                high, edge_low = lax.optimization_barrier((high, edge_low))
            if last and view + 1 == views:
                one, kept, corr = call(
                    far_last_kernel, [piece, piece, packed], low, high, main, mat_ya, back_x,
                    scratch=[pltpu.VMEM(field, F32)],
                )
                (window,) = call(
                    near_last_kernel, [edge], edge_low, edge_high, corr, window, mat_ya, back_window, cost=10
                )
                break
            old_back_x, old_back_window, old_ya = back_x, back_window, mat_ya
            if last:
                back_x, back_window, mat_x, around, mat_y, mat_ya, k_z = next_mats
            main, corr, part = call(
                far_kernel, [field, packed, field], low, high, main, old_ya, old_back_x, mat_x, mat_y, cost=1
            )
            if ahead and last:
                corr, next_two = lax.optimization_barrier((corr, next_two))
                image = next_one, next_two, next_kept
            elif ahead:
                corr, next_one = lax.optimization_barrier((corr, next_one))
            window, part, sent_core, *sent_planes = call(
                near_kernel, [packed, by_half, sent_both, sent, sent],
                edge_low, edge_high, corr, window, part, old_ya, old_back_window, mat_y, around,
            )
    (out,) = call(
        leave_kernel, [estimate_start.shape],
        send(one, back(entry_one(n))), send(kept, entry_two(n, True)), kept, send(window, entry_two(n, True)), window,
    )
    return out


def solution(mesh):
    return jax.shard_map(
        local,
        mesh=mesh,
        in_specs=(P(("grp", "gz"), "gy", None), P(None, ("grp", "gz"), "gy", None), P()),
        out_specs=P(("grp", "gz"), "gy", None),
        check_vma=False,
    )
```

profile of v0, /device:TPU:1, one launch (start us, length us, event | category | flops | bytes accessed | tf_op | source)
XLA Modules:
  0.0 209.1 jit_solution(1121667714717537992)
XLA Ops:
  1.3 2.7 %collective-permute-start.1 = (f32[20,32,128]{2,1,0:T(8,128)S(1)}, f32[20,32,128]{2,1,0:T(8,128)S(1)}, u32[]{:S(2)}, u32[]{:S(2)}) collective-permute-start(f32[20,32,128]{2,1,0:T(8,128)S(1)} %get-tuple-element.250.kept_ref), channel_id=1, source_target_pairs={{1,2},{2,1},{0,4},{3,7},{5,6},{6,5},{4,0},{7,3},{9,10},{10,9},{8,1... | collective-permute-start | bytes 983048 | tf_op jit(solution)/shard_map/ppermute | solution.py:466
  8.7 2.3 %collective-permute-done.1.two_ref = f32[20,32,128]{2,1,0:T(8,128)S(1)} collective-permute-done((f32[20,32,128]{2,1,0:T(8,128)S(1)}, f32[20,32,128]{2,1,0:T(8,128)S(1)}, u32[]{:S(2)}, u32[]{:S(2)}) %collective-permute-start.1) | collective-permute-done | bytes 327712 | tf_op jit(solution)/shard_map/ppermute | solution.py:466
  11.0 2.4 %collective-permute-done.one_ref = f32[20,32,128]{2,1,0:T(8,128)S(1)} collective-permute-done((f32[20,32,128]{2,1,0:T(8,128)S(1)}, f32[20,32,128]{2,1,0:T(8,128)S(1)}, u32[]{:S(2)}, u32[]{:S(2)}) %collective-permute-start) | collective-permute-done | bytes 327712 | tf_op jit(solution)/shard_map/ppermute | solution.py:466
  18.6 4.6 %collective-permute-done.6.one_ref = f32[16,32,128]{2,1,0:T(8,128)S(1)} collective-permute-done((f32[16,32,128]{2,1,0:T(8,128)S(1)}, f32[16,32,128]{2,1,0:T(8,128)S(1)}, u32[]{:S(2)}, u32[]{:S(2)}) %collective-permute-start.6) | collective-permute-done | bytes 262176 | tf_op jit(solution)/shard_map/ppermute | solution.py:466
  28.1 2.0 collective-permute-done.9.chip_ref
  31.2 1.9 collective-permute-done.12.chip_ref
  34.9 2.5 %shard_map.48 = (f32[16,64,128]{2,1,0:T(8,128)S(1)}, f32[256,128]{1,0:T(8,128)S(1)}, f32[16,64,128]{2,1,0:T(8,128)S(1)}) custom-call(f32[16,32,128]{2,1,0:T(8,128)S(1)} %get-tuple-element.276.low_ref, f32[16,32,128]{2,1,0:T(8,128)S(1)} %get-tuple-element.280.high_ref, f32[16,64,128]{2,1,0:T(8,128)S(1)} %get-tuple-element.281.est_ref, ...), custom_call_target="tpu_custom_call" | custom-call | flops 1000000000 | bytes 3000001 | tf_op jit(solution)/shard_map/pallas_call | solution.py:110
  43.5 3.2 %collective-permute-done.16.chip_ref = f32[15,32,128]{2,1,0:T(8,128)S(1)} collective-permute-done((f32[15,32,128]{2,1,0:T(8,128)S(1)}, f32[15,32,128]{2,1,0:T(8,128)S(1)}, u32[]{:S(2)}, u32[]{:S(2)}) %collective-permute-start.16) | collective-permute-done | bytes 245792 | tf_op jit(solution)/shard_map/ppermute | solution.py:466
  53.5 2.0 collective-permute-start.24
  57.9 2.5 %shard_map.57 = (f32[16,64,128]{2,1,0:T(8,128)S(1)}, f32[256,128]{1,0:T(8,128)S(1)}, f32[16,64,128]{2,1,0:T(8,128)S(1)}) custom-call(f32[16,32,128]{2,1,0:T(8,128)S(1)} %get-tuple-element.302.low_ref, f32[16,32,128]{2,1,0:T(8,128)S(1)} %get-tuple-element.306.high_ref, f32[16,64,128]{2,1,0:T(8,128)S(1)} %get-tuple-element.307.est_ref, ...), custom_call_target="tpu_custom_call" | custom-call | flops 1000000000 | bytes 3000001 | tf_op jit(solution)/shard_map/pallas_call | solution.py:110
  67.2 3.2 %collective-permute-done.26.chip_ref = f32[15,32,128]{2,1,0:T(8,128)S(1)} collective-permute-done((f32[15,32,128]{2,1,0:T(8,128)S(1)}, f32[15,32,128]{2,1,0:T(8,128)S(1)}, u32[]{:S(2)}, u32[]{:S(2)}) %collective-permute-start.26) | collective-permute-done | bytes 245792 | tf_op jit(solution)/shard_map/ppermute | solution.py:466
  74.3 1.8 collective-permute-start.32
  78.1 2.1 %collective-permute-done.32.chip_ref = f32[15,32,128]{2,1,0:T(8,128)S(1)} collective-permute-done((f32[15,32,128]{2,1,0:T(8,128)S(1)}, f32[15,32,128]{2,1,0:T(8,128)S(1)}, u32[]{:S(2)}, u32[]{:S(2)}) %collective-permute-start.32) | collective-permute-done | bytes 245792 | tf_op jit(solution)/shard_map/ppermute | solution.py:466
  82.1 2.5 %shard_map.67 = (f32[16,64,128]{2,1,0:T(8,128)S(1)}, f32[256,128]{1,0:T(8,128)S(1)}, f32[16,64,128]{2,1,0:T(8,128)S(1)}) custom-call(f32[16,32,128]{2,1,0:T(8,128)S(1)} %get-tuple-element.338.low_ref, f32[16,32,128]{2,1,0:T(8,128)S(1)} %get-tuple-element.342.high_ref, f32[16,64,128]{2,1,0:T(8,128)S(1)} %get-tuple-element.343.est_ref, ...), custom_call_target="tpu_custom_call" | custom-call | flops 1000000000 | bytes 3000001 | tf_op jit(solution)/shard_map/pallas_call | solution.py:110
  86.0 2.2 %collective-permute-start.35 = (f32[2,15,32,128]{3,2,1,0:T(8,128)S(1)}, f32[2,15,32,128]{3,2,1,0:T(8,128)S(1)}, u32[]{:S(2)}, u32[]{:S(2)}) collective-permute-start(f32[2,15,32,128]{3,2,1,0:T(8,128)S(1)} %get-tuple-element.354), channel_id=1, source_target_pairs={{0,1},{1,0},{2,3},{3,2},{4,5},{5,4},{6,7},{7,6},{8,9},{9,8},{10,11... | collective-permute-start | bytes 1474568 | tf_op jit(solution)/shard_map/ppermute | solution.py:466
  90.9 3.2 %collective-permute-done.36.chip_ref = f32[15,32,128]{2,1,0:T(8,128)S(1)} collective-permute-done((f32[15,32,128]{2,1,0:T(8,128)S(1)}, f32[15,32,128]{2,1,0:T(8,128)S(1)}, u32[]{:S(2)}, u32[]{:S(2)}) %collective-permute-start.36) | collective-permute-done | bytes 245792 | tf_op jit(solution)/shard_map/ppermute | solution.py:466
  98.8 1.8 collective-permute-done.38.chip_ref
  105.1 2.5 %shard_map.76 = (f32[16,64,128]{2,1,0:T(8,128)S(1)}, f32[256,128]{1,0:T(8,128)S(1)}, f32[16,64,128]{2,1,0:T(8,128)S(1)}) custom-call(f32[16,32,128]{2,1,0:T(8,128)S(1)} %get-tuple-element.364.low_ref, f32[16,32,128]{2,1,0:T(8,128)S(1)} %get-tuple-element.368.high_ref, f32[16,64,128]{2,1,0:T(8,128)S(1)} %get-tuple-element.369.est_ref, ...), custom_call_target="tpu_custom_call" | custom-call | flops 1000000000 | bytes 3000001 | tf_op jit(solution)/shard_map/pallas_call | solution.py:110
  114.4 3.2 %collective-permute-done.47.chip_ref = f32[15,32,128]{2,1,0:T(8,128)S(1)} collective-permute-done((f32[15,32,128]{2,1,0:T(8,128)S(1)}, f32[15,32,128]{2,1,0:T(8,128)S(1)}, u32[]{:S(2)}, u32[]{:S(2)}) %collective-permute-start.47) | collective-permute-done | bytes 245792 | tf_op jit(solution)/shard_map/ppermute | solution.py:466
  128.9 2.5 %shard_map.86 = (f32[16,64,128]{2,1,0:T(8,128)S(1)}, f32[256,128]{1,0:T(8,128)S(1)}, f32[16,64,128]{2,1,0:T(8,128)S(1)}) custom-call(f32[16,32,128]{2,1,0:T(8,128)S(1)} %get-tuple-element.402.low_ref, f32[16,32,128]{2,1,0:T(8,128)S(1)} %get-tuple-element.406.high_ref, f32[16,64,128]{2,1,0:T(8,128)S(1)} %get-tuple-element.407.est_ref, ...), custom_call_target="tpu_custom_call" | custom-call | flops 1000000000 | bytes 3000001 | tf_op jit(solution)/shard_map/pallas_call | solution.py:110
  137.4 3.2 %collective-permute-done.56.chip_ref = f32[15,32,128]{2,1,0:T(8,128)S(1)} collective-permute-done((f32[15,32,128]{2,1,0:T(8,128)S(1)}, f32[15,32,128]{2,1,0:T(8,128)S(1)}, u32[]{:S(2)}, u32[]{:S(2)}) %collective-permute-start.56) | collective-permute-done | bytes 245792 | tf_op jit(solution)/shard_map/ppermute | solution.py:466
  145.0 2.1 collective-permute-done.58.chip_ref
  147.4 2.0 collective-permute-start.64
  152.1 2.5 %shard_map.95 = (f32[16,64,128]{2,1,0:T(8,128)S(1)}, f32[256,128]{1,0:T(8,128)S(1)}, f32[16,64,128]{2,1,0:T(8,128)S(1)}) custom-call(f32[16,32,128]{2,1,0:T(8,128)S(1)} %get-tuple-element.428.low_ref, f32[16,32,128]{2,1,0:T(8,128)S(1)} %get-tuple-element.432.high_ref, f32[16,64,128]{2,1,0:T(8,128)S(1)} %get-tuple-element.433.est_ref, ...), custom_call_target="tpu_custom_call" | custom-call | flops 1000000000 | bytes 3000001 | tf_op jit(solution)/shard_map/pallas_call | solution.py:110
  161.1 3.2 %collective-permute-done.67.chip_ref = f32[15,32,128]{2,1,0:T(8,128)S(1)} collective-permute-done((f32[15,32,128]{2,1,0:T(8,128)S(1)}, f32[15,32,128]{2,1,0:T(8,128)S(1)}, u32[]{:S(2)}, u32[]{:S(2)}) %collective-permute-start.67) | collective-permute-done | bytes 245792 | tf_op jit(solution)/shard_map/ppermute | solution.py:466
  168.2 2.6 %collective-permute-done.70.chip_ref = f32[15,32,128]{2,1,0:T(8,128)S(1)} collective-permute-done((f32[15,32,128]{2,1,0:T(8,128)S(1)}, f32[15,32,128]{2,1,0:T(8,128)S(1)}, u32[]{:S(2)}, u32[]{:S(2)}) %collective-permute-start.70) | collective-permute-done | bytes 245792 | tf_op jit(solution)/shard_map/ppermute | solution.py:466
  175.0 2.5 %shard_map.104 = (f32[16,64,128]{2,1,0:T(8,128)S(1)}, f32[256,128]{1,0:T(8,128)S(1)}, f32[16,64,128]{2,1,0:T(8,128)S(1)}) custom-call(f32[16,32,128]{2,1,0:T(8,128)S(1)} %get-tuple-element.455.low_ref, f32[16,32,128]{2,1,0:T(8,128)S(1)} %get-tuple-element.462.high_ref, f32[16,64,128]{2,1,0:T(8,128)S(1)} %get-tuple-element.463.est_ref, ...), custom_call_target="tpu_custom_call" | custom-call | flops 1000000000 | bytes 3000001 | tf_op jit(solution)/shard_map/pallas_call | solution.py:110
  182.6 3.2 %collective-permute-done.75.chip_ref = f32[15,32,128]{2,1,0:T(8,128)S(1)} collective-permute-done((f32[15,32,128]{2,1,0:T(8,128)S(1)}, f32[15,32,128]{2,1,0:T(8,128)S(1)}, u32[]{:S(2)}, u32[]{:S(2)}) %collective-permute-start.75) | collective-permute-done | bytes 245792 | tf_op jit(solution)/shard_map/ppermute | solution.py:466
  186.4 2.0 collective-permute-done.78.chip_ref
  189.5 2.8 %collective-permute-done.77.chip_ref = f32[15,32,128]{2,1,0:T(8,128)S(1)} collective-permute-done((f32[15,32,128]{2,1,0:T(8,128)S(1)}, f32[15,32,128]{2,1,0:T(8,128)S(1)}, u32[]{:S(2)}, u32[]{:S(2)}) %collective-permute-start.77) | collective-permute-done | bytes 245792 | tf_op jit(solution)/shard_map/ppermute | solution.py:466
  198.6 2.0 collective-permute-start.83
  201.6 6.6 %collective-permute-done.85.window_ref = f32[4,32,128]{2,1,0:T(8,128)S(1)} collective-permute-done((f32[4,32,128]{2,1,0:T(8,128)S(1)}, f32[4,32,128]{2,1,0:T(8,128)S(1)}, u32[]{:S(2)}, u32[]{:S(2)}) %collective-permute-start.85) | collective-permute-done | bytes 65568 | tf_op jit(solution)/shard_map/ppermute | solution.py:466
  (228 shorter events, 123.2 us)
Async XLA Ops:
  1.3 9.7 %collective-permute-start.1 = (f32[20,32,128]{2,1,0:T(8,128)S(1)}, f32[20,32,128]{2,1,0:T(8,128)S(1)}, u32[]{:S(2)}, u32[]{:S(2)}) collective-permute-start(f32[20,32,128]{2,1,0:T(8,128)S(1)} %get-tuple-element.250.kept_ref), channel_id=1, source_target_pairs={{1,2},{2,1},{0,4},{3,7},{5,6},{6,5},{4,0},{7,3},{9,10},{10,9},{8,1... | collective-permute-start | bytes 983048 | tf_op jit(solution)/shard_map/ppermute | solution.py:466
  3.9 9.5 %collective-permute-start = (f32[20,32,128]{2,1,0:T(8,128)S(1)}, f32[20,32,128]{2,1,0:T(8,128)S(1)}, u32[]{:S(2)}, u32[]{:S(2)}) collective-permute-start(f32[20,32,128]{2,1,0:T(8,128)S(1)} %get-tuple-element.249), channel_id=1, source_target_pairs={{1,0},{0,2},{2,3},{3,1},{5,4},{4,6},{6,7},{7,5},{9,8},{8,10},{10,1... | collective-permute-start | bytes 983048 | tf_op jit(solution)/shard_map/ppermute | solution.py:466
  5.5 13.2 %collective-permute-start.7 = (f32[16,32,128]{2,1,0:T(8,128)S(1)}, f32[16,32,128]{2,1,0:T(8,128)S(1)}, u32[]{:S(2)}, u32[]{:S(2)}) collective-permute-start(f32[16,32,128]{2,1,0:T(8,128)S(1)} %get-tuple-element.499.kept_ref), channel_id=1, source_target_pairs={{1,2},{2,1},{0,3},{3,0},{5,6},{6,5},{4,7},{7,4},{9,10},{10,9},{8,1... | collective-permute-start | bytes 786440 | tf_op jit(solution)/shard_map/ppermute | solution.py:466
  6.2 17.1 %collective-permute-start.6 = (f32[16,32,128]{2,1,0:T(8,128)S(1)}, f32[16,32,128]{2,1,0:T(8,128)S(1)}, u32[]{:S(2)}, u32[]{:S(2)}) collective-permute-start(f32[16,32,128]{2,1,0:T(8,128)S(1)} %get-tuple-element.500), channel_id=1, source_target_pairs={{1,0},{0,2},{2,3},{3,1},{5,4},{4,6},{6,7},{7,5},{9,8},{8,10},{10,1... | collective-permute-start | bytes 786440 | tf_op jit(solution)/shard_map/ppermute | solution.py:466
  15.3 8.0 %collective-permute-start.5 = (f32[15,32,128]{2,1,0:T(8,128)S(1)}, f32[15,32,128]{2,1,0:T(8,128)S(1)}, u32[]{:S(2)}, u32[]{:S(2)}) collective-permute-start(f32[15,32,128]{2,1,0:T(8,128)S(1)} %get-tuple-element.267), channel_id=1, source_target_pairs={{1,4},{4,1},{5,8},{8,5},{9,12},{12,9},{0,2},{13,15},{3,6},{6,3},{7... | collective-permute-start | bytes 737288 | tf_op jit(solution)/shard_map/ppermute | solution.py:466
  16.5 8.9 %collective-permute-start.2 = (f32[15,32,128]{2,1,0:T(8,128)S(1)}, f32[15,32,128]{2,1,0:T(8,128)S(1)}, u32[]{:S(2)}, u32[]{:S(2)}) collective-permute-start(f32[15,32,128]{2,1,0:T(8,128)S(1)} %get-tuple-element.254), channel_id=1, source_target_pairs={{1,4},{4,1},{5,8},{8,5},{9,12},{12,9},{0,2},{13,15},{3,6},{6,3},{7... | collective-permute-start | bytes 737288 | tf_op jit(solution)/shard_map/ppermute | solution.py:466
  30.4 7.0 %collective-permute-start.14 = (f32[16,32,128]{2,1,0:T(8,128)S(1)}, f32[16,32,128]{2,1,0:T(8,128)S(1)}, u32[]{:S(2)}, u32[]{:S(2)}) collective-permute-start(f32[16,32,128]{2,1,0:T(8,128)S(1)} %get-tuple-element.286), channel_id=1, source_target_pairs={{1,0},{0,2},{2,3},{3,1},{5,4},{4,6},{6,7},{7,5},{9,8},{8,10},{10,1... | collective-permute-start | bytes 786440 | tf_op jit(solution)/shard_map/ppermute | solution.py:466
  40.8 5.9 %collective-permute-start.16 = (f32[15,32,128]{2,1,0:T(8,128)S(1)}, f32[15,32,128]{2,1,0:T(8,128)S(1)}, u32[]{:S(2)}, u32[]{:S(2)}) collective-permute-start(f32[15,32,128]{2,1,0:T(8,128)S(1)} %get-tuple-element.293), channel_id=1, source_target_pairs={{1,4},{4,1},{5,8},{8,5},{9,12},{12,9},{0,2},{13,15},{3,6},{6,3},{7... | collective-permute-start | bytes 737288 | tf_op jit(solution)/shard_map/ppermute | solution.py:466
  41.3 7.9 %collective-permute-start.20 = (f32[15,32,128]{2,1,0:T(8,128)S(1)}, f32[15,32,128]{2,1,0:T(8,128)S(1)}, u32[]{:S(2)}, u32[]{:S(2)}) collective-permute-start(f32[15,32,128]{2,1,0:T(8,128)S(1)} %get-tuple-element.298), channel_id=1, source_target_pairs={{1,4},{4,1},{5,8},{8,5},{9,12},{12,9},{0,2},{13,15},{3,6},{6,3},{7... | collective-permute-start | bytes 737288 | tf_op jit(solution)/shard_map/ppermute | solution.py:466
  47.3 5.9 %collective-permute-start.18 = (f32[15,32,128]{2,1,0:T(8,128)S(1)}, f32[15,32,128]{2,1,0:T(8,128)S(1)}, u32[]{:S(2)}, u32[]{:S(2)}) collective-permute-start(f32[15,32,128]{2,1,0:T(8,128)S(1)} %get-tuple-element.296), channel_id=1, source_target_pairs={{1,4},{4,1},{5,8},{8,5},{9,12},{12,9},{0,2},{13,15},{3,6},{6,3},{7... | collective-permute-start | bytes 737288 | tf_op jit(solution)/shard_map/ppermute | solution.py:466
  49.6 5.9 %collective-permute-start.21 = (f32[15,32,128]{2,1,0:T(8,128)S(1)}, f32[15,32,128]{2,1,0:T(8,128)S(1)}, u32[]{:S(2)}, u32[]{:S(2)}) collective-permute-start(f32[15,32,128]{2,1,0:T(8,128)S(1)} %get-tuple-element.301), channel_id=1, source_target_pairs={{0,1},{1,0},{2,3},{3,2},{4,5},{5,4},{6,7},{7,6},{8,9},{9,8},{10,11... | collective-permute-start | bytes 737288 | tf_op jit(solution)/shard_map/ppermute | solution.py:466
  49.9 6.1 %collective-permute-start.22 = (f32[15,32,128]{2,1,0:T(8,128)S(1)}, f32[15,32,128]{2,1,0:T(8,128)S(1)}, u32[]{:S(2)}, u32[]{:S(2)}) collective-permute-start(f32[15,32,128]{2,1,0:T(8,128)S(1)} %get-tuple-element.304), channel_id=1, source_target_pairs={{1,4},{4,1},{5,8},{8,5},{9,12},{12,9},{0,2},{13,15},{3,6},{6,3},{7... | collective-permute-start | bytes 737288 | tf_op jit(solution)/shard_map/ppermute | solution.py:466
  53.5 6.9 %collective-permute-start.24 = (f32[16,32,128]{2,1,0:T(8,128)S(1)}, f32[16,32,128]{2,1,0:T(8,128)S(1)}, u32[]{:S(2)}, u32[]{:S(2)}) collective-permute-start(f32[16,32,128]{2,1,0:T(8,128)S(1)} %get-tuple-element.312.kept_ref), channel_id=1, source_target_pairs={{1,2},{2,1},{0,4},{3,7},{5,6},{6,5},{4,0},{7,3},{9,10},{10,9},{8,1... | collective-permute-start | bytes 786440 | tf_op jit(solution)/shard_map/ppermute | solution.py:466
  64.4 5.9 %collective-permute-start.26 = (f32[15,32,128]{2,1,0:T(8,128)S(1)}, f32[15,32,128]{2,1,0:T(8,128)S(1)}, u32[]{:S(2)}, u32[]{:S(2)}) collective-permute-start(f32[15,32,128]{2,1,0:T(8,128)S(1)} %get-tuple-element.319), channel_id=1, source_target_pairs={{1,4},{4,1},{5,8},{8,5},{9,12},{12,9},{0,2},{13,15},{3,6},{6,3},{7... | collective-permute-start | bytes 737288 | tf_op jit(solution)/shard_map/ppermute | solution.py:466
  65.8 7.9 %collective-permute-start.30 = (f32[15,32,128]{2,1,0:T(8,128)S(1)}, f32[15,32,128]{2,1,0:T(8,128)S(1)}, u32[]{:S(2)}, u32[]{:S(2)}) collective-permute-start(f32[15,32,128]{2,1,0:T(8,128)S(1)} %get-tuple-element.326), channel_id=1, source_target_pairs={{1,4},{4,1},{5,8},{8,5},{9,12},{12,9},{0,2},{13,15},{3,6},{6,3},{7... | collective-permute-start | bytes 737288 | tf_op jit(solution)/shard_map/ppermute | solution.py:466
  71.0 5.9 %collective-permute-start.28 = (f32[15,32,128]{2,1,0:T(8,128)S(1)}, f32[15,32,128]{2,1,0:T(8,128)S(1)}, u32[]{:S(2)}, u32[]{:S(2)}) collective-permute-start(f32[15,32,128]{2,1,0:T(8,128)S(1)} %get-tuple-element.324), channel_id=1, source_target_pairs={{1,4},{4,1},{5,8},{8,5},{9,12},{12,9},{0,2},{13,15},{3,6},{6,3},{7... | collective-permute-start | bytes 737288 | tf_op jit(solution)/shard_map/ppermute | solution.py:466
  74.3 5.9 %collective-permute-start.32 = (f32[15,32,128]{2,1,0:T(8,128)S(1)}, f32[15,32,128]{2,1,0:T(8,128)S(1)}, u32[]{:S(2)}, u32[]{:S(2)}) collective-permute-start(f32[15,32,128]{2,1,0:T(8,128)S(1)} %get-tuple-element.340), channel_id=1, source_target_pairs={{1,4},{4,1},{5,8},{8,5},{9,12},{12,9},{0,2},{13,15},{3,6},{6,3},{7... | collective-permute-start | bytes 737288 | tf_op jit(solution)/shard_map/ppermute | solution.py:466
  77.2 7.4 %collective-permute-start.34 = (f32[16,32,128]{2,1,0:T(8,128)S(1)}, f32[16,32,128]{2,1,0:T(8,128)S(1)}, u32[]{:S(2)}, u32[]{:S(2)}) collective-permute-start(f32[16,32,128]{2,1,0:T(8,128)S(1)} %get-tuple-element.348), channel_id=1, source_target_pairs={{1,0},{0,2},{2,3},{3,1},{5,4},{4,6},{6,7},{7,5},{9,8},{8,10},{10,1... | collective-permute-start | bytes 786440 | tf_op jit(solution)/shard_map/ppermute | solution.py:466
  88.2 5.9 %collective-permute-start.36 = (f32[15,32,128]{2,1,0:T(8,128)S(1)}, f32[15,32,128]{2,1,0:T(8,128)S(1)}, u32[]{:S(2)}, u32[]{:S(2)}) collective-permute-start(f32[15,32,128]{2,1,0:T(8,128)S(1)} %get-tuple-element.355), channel_id=1, source_target_pairs={{1,4},{4,1},{5,8},{8,5},{9,12},{12,9},{0,2},{13,15},{3,6},{6,3},{7... | collective-permute-start | bytes 737288 | tf_op jit(solution)/shard_map/ppermute | solution.py:466
  89.2 7.5 %collective-permute-start.40 = (f32[15,32,128]{2,1,0:T(8,128)S(1)}, f32[15,32,128]{2,1,0:T(8,128)S(1)}, u32[]{:S(2)}, u32[]{:S(2)}) collective-permute-start(f32[15,32,128]{2,1,0:T(8,128)S(1)} %get-tuple-element.360), channel_id=1, source_target_pairs={{1,4},{4,1},{5,8},{8,5},{9,12},{12,9},{0,2},{13,15},{3,6},{6,3},{7... | collective-permute-start | bytes 737288 | tf_op jit(solution)/shard_map/ppermute | solution.py:466
  94.7 5.9 %collective-permute-start.38 = (f32[15,32,128]{2,1,0:T(8,128)S(1)}, f32[15,32,128]{2,1,0:T(8,128)S(1)}, u32[]{:S(2)}, u32[]{:S(2)}) collective-permute-start(f32[15,32,128]{2,1,0:T(8,128)S(1)} %get-tuple-element.358), channel_id=1, source_target_pairs={{1,4},{4,1},{5,8},{8,5},{9,12},{12,9},{0,2},{13,15},{3,6},{6,3},{7... | collective-permute-start | bytes 737288 | tf_op jit(solution)/shard_map/ppermute | solution.py:466
  97.3 5.9 %collective-permute-start.42 = (f32[15,32,128]{2,1,0:T(8,128)S(1)}, f32[15,32,128]{2,1,0:T(8,128)S(1)}, u32[]{:S(2)}, u32[]{:S(2)}) collective-permute-start(f32[15,32,128]{2,1,0:T(8,128)S(1)} %get-tuple-element.366), channel_id=1, source_target_pairs={{1,4},{4,1},{5,8},{8,5},{9,12},{12,9},{0,2},{13,15},{3,6},{6,3},{7... | collective-permute-start | bytes 737288 | tf_op jit(solution)/shard_map/ppermute | solution.py:466
  100.9 6.7 %collective-permute-start.44 = (f32[16,32,128]{2,1,0:T(8,128)S(1)}, f32[16,32,128]{2,1,0:T(8,128)S(1)}, u32[]{:S(2)}, u32[]{:S(2)}) collective-permute-start(f32[16,32,128]{2,1,0:T(8,128)S(1)} %get-tuple-element.374.kept_ref), channel_id=1, source_target_pairs={{1,2},{2,1},{0,4},{3,7},{5,6},{6,5},{4,0},{7,3},{9,10},{10,9},{8,1... | collective-permute-start | bytes 786440 | tf_op jit(solution)/shard_map/ppermute | solution.py:466
  112.6 7.9 %collective-permute-start.45 = (f32[15,32,128]{2,1,0:T(8,128)S(1)}, f32[15,32,128]{2,1,0:T(8,128)S(1)}, u32[]{:S(2)}, u32[]{:S(2)}) collective-permute-start(f32[15,32,128]{2,1,0:T(8,128)S(1)} %get-tuple-element.379), channel_id=1, source_target_pairs={{1,4},{4,1},{5,8},{8,5},{9,12},{12,9},{0,2},{13,15},{3,6},{6,3},{7... | collective-permute-start | bytes 737288 | tf_op jit(solution)/shard_map/ppermute | solution.py:466
  124.4 6.9 %collective-permute-start.54 = (f32[16,32,128]{2,1,0:T(8,128)S(1)}, f32[16,32,128]{2,1,0:T(8,128)S(1)}, u32[]{:S(2)}, u32[]{:S(2)}) collective-permute-start(f32[16,32,128]{2,1,0:T(8,128)S(1)} %get-tuple-element.412), channel_id=1, source_target_pairs={{1,0},{0,2},{2,3},{3,1},{5,4},{4,6},{6,7},{7,5},{9,8},{8,10},{10,1... | collective-permute-start | bytes 786440 | tf_op jit(solution)/shard_map/ppermute | solution.py:466
  135.3 7.9 %collective-permute-start.60 = (f32[15,32,128]{2,1,0:T(8,128)S(1)}, f32[15,32,128]{2,1,0:T(8,128)S(1)}, u32[]{:S(2)}, u32[]{:S(2)}) collective-permute-start(f32[15,32,128]{2,1,0:T(8,128)S(1)} %get-tuple-element.424), channel_id=1, source_target_pairs={{1,4},{4,1},{5,8},{8,5},{9,12},{12,9},{0,2},{13,15},{3,6},{6,3},{7... | collective-permute-start | bytes 737288 | tf_op jit(solution)/shard_map/ppermute | solution.py:466
  147.4 7.1 %collective-permute-start.64 = (f32[16,32,128]{2,1,0:T(8,128)S(1)}, f32[16,32,128]{2,1,0:T(8,128)S(1)}, u32[]{:S(2)}, u32[]{:S(2)}) collective-permute-start(f32[16,32,128]{2,1,0:T(8,128)S(1)} %get-tuple-element.438.kept_ref), channel_id=1, source_target_pairs={{1,2},{2,1},{0,4},{3,7},{5,6},{6,5},{4,0},{7,3},{9,10},{10,9},{8,1... | collective-permute-start | bytes 786440 | tf_op jit(solution)/shard_map/ppermute | solution.py:466
  158.6 8.3 %collective-permute-start.66 = (f32[15,32,128]{2,1,0:T(8,128)S(1)}, f32[15,32,128]{2,1,0:T(8,128)S(1)}, u32[]{:S(2)}, u32[]{:S(2)}) collective-permute-start(f32[15,32,128]{2,1,0:T(8,128)S(1)} %get-tuple-element.445), channel_id=1, source_target_pairs={{1,4},{4,1},{5,8},{8,5},{9,12},{12,9},{0,2},{13,15},{3,6},{6,3},{7... | collective-permute-start | bytes 737288 | tf_op jit(solution)/shard_map/ppermute | solution.py:466
  179.9 8.5 %collective-permute-start.78 = (f32[15,32,128]{2,1,0:T(8,128)S(1)}, f32[15,32,128]{2,1,0:T(8,128)S(1)}, u32[]{:S(2)}, u32[]{:S(2)}) collective-permute-start(f32[15,32,128]{2,1,0:T(8,128)S(1)} %get-tuple-element.477), channel_id=1, source_target_pairs={{1,4},{4,1},{5,8},{8,5},{9,12},{12,9},{0,2},{13,15},{3,6},{6,3},{7... | collective-permute-start | bytes 737288 | tf_op jit(solution)/shard_map/ppermute | solution.py:466
  198.1 10.1 %collective-permute-start.82 = (f32[16,32,128]{2,1,0:T(8,128)S(1)}, f32[16,32,128]{2,1,0:T(8,128)S(1)}, u32[]{:S(2)}, u32[]{:S(2)}) collective-permute-start(f32[16,32,128]{2,1,0:T(8,128)S(1)} %get-tuple-element.487), channel_id=1, source_target_pairs={{0,1},{2,0},{3,2},{1,3},{4,5},{6,4},{7,6},{5,7},{8,9},{10,8},{11,1... | collective-permute-start | bytes 786440 | tf_op jit(solution)/shard_map/ppermute | solution.py:466
  198.6 9.6 %collective-permute-start.83 = (f32[16,32,128]{2,1,0:T(8,128)S(1)}, f32[16,32,128]{2,1,0:T(8,128)S(1)}, u32[]{:S(2)}, u32[]{:S(2)}) collective-permute-start(f32[16,32,128]{2,1,0:T(8,128)S(1)} %get-tuple-element.488.kept_ref), channel_id=1, source_target_pairs={{1,2},{2,1},{0,4},{3,7},{5,6},{6,5},{4,0},{7,3},{9,10},{10,9},{8,1... | collective-permute-start | bytes 786440 | tf_op jit(solution)/shard_map/ppermute | solution.py:466
  201.1 7.1 %collective-permute-start.85 = (f32[4,32,128]{2,1,0:T(8,128)S(1)}, f32[4,32,128]{2,1,0:T(8,128)S(1)}, u32[]{:S(2)}, u32[]{:S(2)}) collective-permute-start(f32[4,32,128]{2,1,0:T(8,128)S(1)} %shard_map.114.window_kept_ref), channel_id=1, source_target_pairs={{1,2},{2,1},{0,4},{3,7},{5,6},{6,5},{4,0},{7,3},{9,10},{10,9},{8,1... | collective-permute-start | bytes 196616 | tf_op jit(solution)/shard_map/ppermute | solution.py:466
  (56 other events, 253.0 us)
where the time goes:
time: 209 us
  waiting for transfers between devices  72.1 us (34%)
  starting transfers between devices  71.8 us (34%)
  Pallas kernels  61.5 us (29%)
  local copies, waits for them, and re-layouts  2.93 us (1%)
    ppermute x86, waiting for transfers between devices, local(): send = lambda value, pairs: lax.ppermute(value, AXES, pairs)  72.1 us
    ppermute x86, starting transfers between devices, local(): send = lambda value, pairs: lax.ppermute(value, AXES, pairs)  71.8 us
    pallas_call x79, Pallas kernels, call(): pl.pallas_call(kernel, out_shape=[jax.ShapeDtypeStruct(s, F32) if isinsta...  61.5 us
  transfers between devices with their start and end apart: 86, of which 40 were waited for; matrix products, arithmetic and copies ran while one was open for 1% of the time, Pallas kernels for 24%

commit v1 on v0

--- a/solution.py
+++ b/solution.py
@@ -94,12 +94,19 @@
 
 def times_right(value, mat_ref):
     high, low = split(value)
-    return dot(high, mat_ref[0]) + (dot(low, mat_ref[0]) + dot(high, mat_ref[1]))
+    if value.shape[1] >= 256:
+        return dot(high, mat_ref[0]) + (dot(low, mat_ref[0]) + dot(high, mat_ref[1]))
+    twice = jnp.concatenate([mat_ref[0], mat_ref[0]], axis=0)
+    return dot(jnp.concatenate([high, low], axis=1), twice) + dot(high, mat_ref[1])
 
 
 def times_left(mat_ref, value):
     high, low = split(value)
-    return dot(mat_ref[0], high) + (dot(mat_ref[0], low) + dot(mat_ref[1], high))
+    cols = value.shape[1]
+    if cols >= 256:
+        return dot(mat_ref[0], high) + (dot(mat_ref[0], low) + dot(mat_ref[1], high))
+    both = dot(mat_ref[0], jnp.concatenate([high, low], axis=1))
+    return both[:, :cols] + (both[:, cols:] + dot(mat_ref[1], high))
 
 
 def call(kernel, outs, *args, scratch=(), cost=0):
@@ -296,6 +303,17 @@
             lax.fori_loop(0, parts * tiles, step, 0)
 
 
+def own_z_mats_kernel(taps, own_ref, core_ref, psf_ref, out_ref, *refs, view, rows):
+    own_z_kernel(taps, own_ref, core_ref, out_ref, flip=False)
+    mats_kernel(psf_ref, *refs, view=view, rows=rows)
+
+
+def own_z_first_mats_kernel(taps, own_ref, core_low_ref, core_high_ref, psf_ref, out_ref, *refs, view, rows):
+    *refs, core_ref = refs
+    own_z_first_kernel(taps, own_ref, core_low_ref, core_high_ref, out_ref, core_ref)
+    mats_kernel(psf_ref, *refs, view=view, rows=rows)
+
+
 def own_z_half_kernel(taps, own_ref, core_ref, out_ref):
     grown = (1, *own_ref.shape)
     own_z_kernel(taps, own_ref.reshape(grown), core_ref.reshape(1, *core_ref.shape), out_ref.reshape(grown), flip=True)
@@ -418,17 +436,13 @@
     window = near_window(edge_low, edge_high, corr_ref, window_ref, mat_ya, mat_window)
     window_out[...] = window
     blurred = times_left(mat_y, window)
-
-    def step(pair, carry):
+    for pair in range(groups // 2):
         share = times_right(blurred, mat_around.at[pair])
         for side in range(2):
-            at = pl.ds(each * (2 * pair + side), each)
+            at = slice(each * (2 * pair + side), each * (2 * pair + side + 1))
             put_rows(
                 part_out, at, part_ref[at] + share[:, cols * side : cols * (side + 1)].reshape(each, rows, cols)
             )
-        return carry
-
-    lax.fori_loop(0, groups // 2, step, 0)
     put_sent(part_out, (core_ref.at[0], core_ref.at[1]), low_ref, high_ref)
 
 
@@ -470,21 +484,17 @@
     sent, by_half = (half, rows_dev, wide), (2, *piece)
     sent_both, edge = (2, *sent), (planes // groups, rows_dev, wide)
 
-    def mats(view):
-        pair = lambda *shape: jax.ShapeDtypeStruct(shape, BF16)
-        return call(
-            functools.partial(mats_kernel, view=view, rows=rows),
-            [
-                pair(groups, 2, wide, 2 * wide),
-                pair(2, wide, wide),
-                pair(2, wide, wide),
-                pair(groups // 2, 2, wide, 2 * wide),
-                pair(2, rows_y, rows_y),
-                pair(2, rows_y, rows_y),
-                (taps, 8, wide),
-            ],
-            psf_taps, scratch=[pltpu.VMEM((cols, cols), F32)] * 2 + [pltpu.VMEM((1, cols), F32)],
-        )
+    pair = lambda *shape: jax.ShapeDtypeStruct(shape, BF16)
+    mats_out = [
+        pair(groups, 2, wide, 2 * wide),
+        pair(2, wide, wide),
+        pair(2, wide, wide),
+        pair(groups // 2, 2, wide, 2 * wide),
+        pair(2, rows_y, rows_y),
+        pair(2, rows_y, rows_y),
+        (taps, 8, wide),
+    ]
+    mats_scratch = [pltpu.VMEM((cols, cols), F32)] * 2 + [pltpu.VMEM((1, cols), F32)]
 
     def pieces(value, *index):
         def cut(half):
@@ -496,7 +506,9 @@
     entry = (planes + planes // groups, rows_dev, wide)
     one, kept = call(cut_kernel, [entry, entry], estimate_start)
     one, two = send(one, entry_one(n)), send(kept, entry_two(n, True))
-    back_x, back_window, mat_x, around, mat_y, mat_ya, k_z = mats(0)
+    back_x, back_window, mat_x, around, mat_y, mat_ya, k_z = call(
+        functools.partial(mats_kernel, view=0, rows=rows), mats_out, psf_taps, scratch=mats_scratch
+    )
     image = pieces(view_images, 0)
     image = send(image[0], entry_one(n)), send(image[1], entry_two(n, False)), image[1]
     main, window, part, core_low, core_high, *sent_planes = call(
@@ -510,18 +522,23 @@
             if ahead and not last:
                 images, _ = lax.optimization_barrier((view_images, part))
                 next_pieces = pieces(images, view + 1)
+            chip = [send(s, chip_swap(n)) for s in sent_planes]
+            name = dict(view=view + 1, rows=rows)
             if view == 0 and step == 0:
-                (own,) = call(
-                    own_z_first_kernel, [by_half], k_z, part,
-                    send(core_low, core_swap(n)), send(core_high, core_swap(n)), scratch=[pltpu.VMEM(sent_both, F32)],
+                own, *next_mats = call(
+                    functools.partial(own_z_first_mats_kernel, **name), [by_half, *mats_out], k_z, part,
+                    send(core_low, core_swap(n)), send(core_high, core_swap(n)), psf_taps,
+                    scratch=mats_scratch + [pltpu.VMEM(sent_both, F32)],
+                )
+            elif ahead and not last:
+                own, *next_mats = call(
+                    functools.partial(own_z_mats_kernel, **name), [by_half, *mats_out], k_z, part,
+                    send(sent_core, core_swap(n)), psf_taps, scratch=mats_scratch,
                 )
             else:
                 (own,) = call(
                     functools.partial(own_z_kernel, flip=False), [by_half], k_z, part, send(sent_core, core_swap(n))
                 )
-            chip = [send(s, chip_swap(n)) for s in sent_planes]
-            if view + 1 < views and not last:
-                chip[1], *next_mats = lax.optimization_barrier((chip[1], *mats(view + 1)))
             ratio, sent_core, sent_low = call(
                 functools.partial(ratio_kernel, side=0), [piece, sent, sent], k_z, own, chip[0], *image
             )

time: 209 us -> 206 us (0.986)
  waiting for transfers between devices: 72.1 us -> 77.6 us
  starting transfers between devices: 71.8 us -> 66.8 us
  Pallas kernels: 61.5 us -> 58.1 us
    ppermute x86, waiting for transfers between devices: 72.1 us -> 77.6 us  [local(): send = lambda value, pairs: lax.ppermute(value, AXES, pairs)]
    ppermute x86, starting transfers between devices: 71.8 us -> 66.8 us  [local(): send = lambda value, pairs: lax.ppermute(value, AXES, pairs)]
    pallas_call x79 -> x76, Pallas kernels: 61.5 us -> 58.1 us  [call(): pl.pallas_call(kernel, out_shape=[jax.ShapeDtypeStruct(s, F32) if isinsta...]
  transfers between devices with their start and end apart: 86 -> 86, of which waited for: 40 -> 40; matrix products, arithmetic and copies ran while one was open for 1% -> 1% of each run, Pallas kernels for 24% -> 25%
where the time goes in v1:
time: 206 us
  waiting for transfers between devices  77.6 us (38%)
  starting transfers between devices  66.8 us (32%)
  Pallas kernels  58.1 us (28%)
  local copies, waits for them, and re-layouts  2.91 us (1%)
    ppermute x86, waiting for transfers between devices, local(): send = lambda value, pairs: lax.ppermute(value, AXES, pairs)  77.6 us
    ppermute x86, starting transfers between devices, local(): send = lambda value, pairs: lax.ppermute(value, AXES, pairs)  66.8 us
    pallas_call x76, Pallas kernels, call(): pl.pallas_call(kernel, out_shape=[jax.ShapeDtypeStruct(s, F32) if isinsta...  58.1 us
  transfers between devices with their start and end apart: 86, of which 40 were waited for; matrix products, arithmetic and copies ran while one was open for 1% of the time, Pallas kernels for 25%

profile of v1, /device:TPU:1, one launch (start us, length us, event | category | flops | bytes accessed | tf_op | source)
XLA Modules:
  0.0 206.1 jit_solution(7179319318330356570)
XLA Ops:
  1.3 2.6 %collective-permute-start.1 = (f32[20,32,128]{2,1,0:T(8,128)S(1)}, f32[20,32,128]{2,1,0:T(8,128)S(1)}, u32[]{:S(2)}, u32[]{:S(2)}) collective-permute-start(f32[20,32,128]{2,1,0:T(8,128)S(1)} %get-tuple-element.230.kept_ref), channel_id=1, source_target_pairs={{1,2},{2,1},{0,4},{3,7},{5,6},{6,5},{4,0},{7,3},{9,10},{10,9},{8,1... | collective-permute-start | bytes 983048 | tf_op jit(solution)/shard_map/ppermute | solution.py:480
  17.0 2.1 %shard_map.40 = (f32[2,16,32,128]{3,2,1,0:T(8,128)S(1)}, bf16[4,2,128,256]{3,2,1,0:T(8,128)(2,1)S(1)}, bf16[2,128,128]{2,1,0:T(8,128)(2,1)S(1)}, bf16[2,128,128]...) custom-call(f32[31,8,128]{2,1,0:T(8,128)S(1)} %get-tuple-element.228, ...), custom_call_target="tpu_custom_call" | custom-call | flops 1 | bytes 1 | tf_op jit(solution)/shard_map/pallas_call | solution.py:117
  20.4 2.9 %collective-permute-start.7 = (f32[15,32,128]{2,1,0:T(8,128)S(1)}, f32[15,32,128]{2,1,0:T(8,128)S(1)}, u32[]{:S(2)}, u32[]{:S(2)}) collective-permute-start(f32[15,32,128]{2,1,0:T(8,128)S(1)} %get-tuple-element.241), channel_id=1, source_target_pairs={{0,1},{1,0},{2,3},{3,2},{4,5},{5,4},{6,7},{7,6},{8,9},{9,8},{10,11... | collective-permute-start | bytes 737288 | tf_op jit(solution)/shard_map/ppermute | solution.py:480
  23.7 2.4 %collective-permute-start.11 = (f32[15,32,128]{2,1,0:T(8,128)S(1)}, f32[15,32,128]{2,1,0:T(8,128)S(1)}, u32[]{:S(2)}, u32[]{:S(2)}) collective-permute-start(f32[15,32,128]{2,1,0:T(8,128)S(1)} %get-tuple-element.247), channel_id=1, source_target_pairs={{0,1},{1,0},{2,3},{3,2},{4,5},{5,4},{6,7},{7,6},{8,9},{9,8},{10,11... | collective-permute-start | bytes 737288 | tf_op jit(solution)/shard_map/ppermute | solution.py:480
  26.6 2.6 %collective-permute-done.8.chip_ref = f32[15,32,128]{2,1,0:T(8,128)S(1)} collective-permute-done((f32[15,32,128]{2,1,0:T(8,128)S(1)}, f32[15,32,128]{2,1,0:T(8,128)S(1)}, u32[]{:S(2)}, u32[]{:S(2)}) %collective-permute-start.8) | collective-permute-done | bytes 245792 | tf_op jit(solution)/shard_map/ppermute | solution.py:480
  34.4 2.5 %shard_map.47 = (f32[16,64,128]{2,1,0:T(8,128)S(1)}, f32[256,128]{1,0:T(8,128)S(1)}, f32[16,64,128]{2,1,0:T(8,128)S(1)}) custom-call(f32[16,32,128]{2,1,0:T(8,128)S(1)} %get-tuple-element.248.low_ref, f32[16,32,128]{2,1,0:T(8,128)S(1)} %get-tuple-element.252.high_ref, f32[16,64,128]{2,1,0:T(8,128)S(1)} %get-tuple-element.253.est_ref, ...), custom_call_target="tpu_custom_call" | custom-call | flops 1000000000 | bytes 3000001 | tf_op jit(solution)/shard_map/pallas_call | solution.py:117
  42.8 3.2 %collective-permute-done.16.chip_ref = f32[15,32,128]{2,1,0:T(8,128)S(1)} collective-permute-done((f32[15,32,128]{2,1,0:T(8,128)S(1)}, f32[15,32,128]{2,1,0:T(8,128)S(1)}, u32[]{:S(2)}, u32[]{:S(2)}) %collective-permute-start.16) | collective-permute-done | bytes 245792 | tf_op jit(solution)/shard_map/ppermute | solution.py:480
  50.3 2.4 %collective-permute-done.18.chip_ref = f32[15,32,128]{2,1,0:T(8,128)S(1)} collective-permute-done((f32[15,32,128]{2,1,0:T(8,128)S(1)}, f32[15,32,128]{2,1,0:T(8,128)S(1)}, u32[]{:S(2)}, u32[]{:S(2)}) %collective-permute-start.18) | collective-permute-done | bytes 245792 | tf_op jit(solution)/shard_map/ppermute | solution.py:480
  53.0 2.1 %collective-permute-start.24 = (f32[16,32,128]{2,1,0:T(8,128)S(1)}, f32[16,32,128]{2,1,0:T(8,128)S(1)}, u32[]{:S(2)}, u32[]{:S(2)}) collective-permute-start(f32[16,32,128]{2,1,0:T(8,128)S(1)} %get-tuple-element.284.kept_ref), channel_id=1, source_target_pairs={{1,2},{2,1},{0,4},{3,7},{5,6},{6,5},{4,0},{7,3},{9,10},{10,9},{8,1... | collective-permute-start | bytes 786440 | tf_op jit(solution)/shard_map/ppermute | solution.py:480
  57.6 2.5 %shard_map.56 = (f32[16,64,128]{2,1,0:T(8,128)S(1)}, f32[256,128]{1,0:T(8,128)S(1)}, f32[16,64,128]{2,1,0:T(8,128)S(1)}) custom-call(f32[16,32,128]{2,1,0:T(8,128)S(1)} %get-tuple-element.274.low_ref, f32[16,32,128]{2,1,0:T(8,128)S(1)} %get-tuple-element.278.high_ref, f32[16,64,128]{2,1,0:T(8,128)S(1)} %get-tuple-element.279.est_ref, ...), custom_call_target="tpu_custom_call" | custom-call | flops 1000000000 | bytes 3000001 | tf_op jit(solution)/shard_map/pallas_call | solution.py:117
  65.4 2.1 %shard_map.58 = (f32[2,16,32,128]{3,2,1,0:T(8,128)S(1)}, bf16[4,2,128,256]{3,2,1,0:T(8,128)(2,1)S(1)}, bf16[2,128,128]{2,1,0:T(8,128)(2,1)S(1)}, bf16[2,128,128]...) custom-call(f32[31,8,128]{2,1,0:T(8,128)S(1)} %get-tuple-element.237, ...), custom_call_target="tpu_custom_call" | custom-call | flops 1 | bytes 1 | tf_op jit(solution)/shard_map/pallas_call | solution.py:117
  67.5 2.1 collective-permute-done.26.chip_ref
  73.5 2.6 %collective-permute-done.28.chip_ref = f32[15,32,128]{2,1,0:T(8,128)S(1)} collective-permute-done((f32[15,32,128]{2,1,0:T(8,128)S(1)}, f32[15,32,128]{2,1,0:T(8,128)S(1)}, u32[]{:S(2)}, u32[]{:S(2)}) %collective-permute-start.28) | collective-permute-done | bytes 245792 | tf_op jit(solution)/shard_map/ppermute | solution.py:480
  80.8 2.5 %shard_map.65 = (f32[16,64,128]{2,1,0:T(8,128)S(1)}, f32[256,128]{1,0:T(8,128)S(1)}, f32[16,64,128]{2,1,0:T(8,128)S(1)}) custom-call(f32[16,32,128]{2,1,0:T(8,128)S(1)} %get-tuple-element.304.low_ref, f32[16,32,128]{2,1,0:T(8,128)S(1)} %get-tuple-element.308.high_ref, f32[16,64,128]{2,1,0:T(8,128)S(1)} %get-tuple-element.309.est_ref, ...), custom_call_target="tpu_custom_call" | custom-call | flops 1000000000 | bytes 3000001 | tf_op jit(solution)/shard_map/pallas_call | solution.py:117
  89.1 3.2 %collective-permute-done.36.chip_ref = f32[15,32,128]{2,1,0:T(8,128)S(1)} collective-permute-done((f32[15,32,128]{2,1,0:T(8,128)S(1)}, f32[15,32,128]{2,1,0:T(8,128)S(1)}, u32[]{:S(2)}, u32[]{:S(2)}) %collective-permute-start.36) | collective-permute-done | bytes 245792 | tf_op jit(solution)/shard_map/ppermute | solution.py:480
  96.1 2.8 %collective-permute-done.38.chip_ref = f32[15,32,128]{2,1,0:T(8,128)S(1)} collective-permute-done((f32[15,32,128]{2,1,0:T(8,128)S(1)}, f32[15,32,128]{2,1,0:T(8,128)S(1)}, u32[]{:S(2)}, u32[]{:S(2)}) %collective-permute-start.38) | collective-permute-done | bytes 245792 | tf_op jit(solution)/shard_map/ppermute | solution.py:480
  99.2 2.1 %collective-permute-start.44 = (f32[16,32,128]{2,1,0:T(8,128)S(1)}, f32[16,32,128]{2,1,0:T(8,128)S(1)}, u32[]{:S(2)}, u32[]{:S(2)}) collective-permute-start(f32[16,32,128]{2,1,0:T(8,128)S(1)} %get-tuple-element.340.kept_ref), channel_id=1, source_target_pairs={{1,2},{2,1},{0,4},{3,7},{5,6},{6,5},{4,0},{7,3},{9,10},{10,9},{8,1... | collective-permute-start | bytes 786440 | tf_op jit(solution)/shard_map/ppermute | solution.py:480
  103.7 2.5 %shard_map.74 = (f32[16,64,128]{2,1,0:T(8,128)S(1)}, f32[256,128]{1,0:T(8,128)S(1)}, f32[16,64,128]{2,1,0:T(8,128)S(1)}) custom-call(f32[16,32,128]{2,1,0:T(8,128)S(1)} %get-tuple-element.330.low_ref, f32[16,32,128]{2,1,0:T(8,128)S(1)} %get-tuple-element.334.high_ref, f32[16,64,128]{2,1,0:T(8,128)S(1)} %get-tuple-element.335.est_ref, ...), custom_call_target="tpu_custom_call" | custom-call | flops 1000000000 | bytes 3000001 | tf_op jit(solution)/shard_map/pallas_call | solution.py:117
  111.5 2.1 %shard_map.76 = (f32[2,16,32,128]{3,2,1,0:T(8,128)S(1)}, bf16[4,2,128,256]{3,2,1,0:T(8,128)(2,1)S(1)}, bf16[2,128,128]{2,1,0:T(8,128)(2,1)S(1)}, bf16[2,128,128]...) custom-call(f32[31,8,128]{2,1,0:T(8,128)S(1)} %get-tuple-element.291, ...), custom_call_target="tpu_custom_call" | custom-call | flops 1 | bytes 1 | tf_op jit(solution)/shard_map/pallas_call | solution.py:117
  113.6 2.1 collective-permute-done.46.chip_ref
  119.5 2.8 %collective-permute-done.48.chip_ref = f32[15,32,128]{2,1,0:T(8,128)S(1)} collective-permute-done((f32[15,32,128]{2,1,0:T(8,128)S(1)}, f32[15,32,128]{2,1,0:T(8,128)S(1)}, u32[]{:S(2)}, u32[]{:S(2)}) %collective-permute-start.48) | collective-permute-done | bytes 245792 | tf_op jit(solution)/shard_map/ppermute | solution.py:480
  126.7 2.5 %shard_map.83 = (f32[16,64,128]{2,1,0:T(8,128)S(1)}, f32[256,128]{1,0:T(8,128)S(1)}, f32[16,64,128]{2,1,0:T(8,128)S(1)}) custom-call(f32[16,32,128]{2,1,0:T(8,128)S(1)} %get-tuple-element.360.low_ref, f32[16,32,128]{2,1,0:T(8,128)S(1)} %get-tuple-element.364.high_ref, f32[16,64,128]{2,1,0:T(8,128)S(1)} %get-tuple-element.365.est_ref, ...), custom_call_target="tpu_custom_call" | custom-call | flops 1000000000 | bytes 3000001 | tf_op jit(solution)/shard_map/pallas_call | solution.py:117
  135.1 3.2 %collective-permute-done.56.chip_ref = f32[15,32,128]{2,1,0:T(8,128)S(1)} collective-permute-done((f32[15,32,128]{2,1,0:T(8,128)S(1)}, f32[15,32,128]{2,1,0:T(8,128)S(1)}, u32[]{:S(2)}, u32[]{:S(2)}) %collective-permute-start.56) | collective-permute-done | bytes 245792 | tf_op jit(solution)/shard_map/ppermute | solution.py:480
  142.2 2.8 %collective-permute-done.58.chip_ref = f32[15,32,128]{2,1,0:T(8,128)S(1)} collective-permute-done((f32[15,32,128]{2,1,0:T(8,128)S(1)}, f32[15,32,128]{2,1,0:T(8,128)S(1)}, u32[]{:S(2)}, u32[]{:S(2)}) %collective-permute-start.58) | collective-permute-done | bytes 245792 | tf_op jit(solution)/shard_map/ppermute | solution.py:480
  145.3 2.1 %collective-permute-start.64 = (f32[16,32,128]{2,1,0:T(8,128)S(1)}, f32[16,32,128]{2,1,0:T(8,128)S(1)}, u32[]{:S(2)}, u32[]{:S(2)}) collective-permute-start(f32[16,32,128]{2,1,0:T(8,128)S(1)} %get-tuple-element.396.kept_ref), channel_id=1, source_target_pairs={{1,2},{2,1},{0,4},{3,7},{5,6},{6,5},{4,0},{7,3},{9,10},{10,9},{8,1... | collective-permute-start | bytes 786440 | tf_op jit(solution)/shard_map/ppermute | solution.py:480
  149.8 2.5 %shard_map.92 = (f32[16,64,128]{2,1,0:T(8,128)S(1)}, f32[256,128]{1,0:T(8,128)S(1)}, f32[16,64,128]{2,1,0:T(8,128)S(1)}) custom-call(f32[16,32,128]{2,1,0:T(8,128)S(1)} %get-tuple-element.386.low_ref, f32[16,32,128]{2,1,0:T(8,128)S(1)} %get-tuple-element.390.high_ref, f32[16,64,128]{2,1,0:T(8,128)S(1)} %get-tuple-element.391.est_ref, ...), custom_call_target="tpu_custom_call" | custom-call | flops 1000000000 | bytes 3000001 | tf_op jit(solution)/shard_map/pallas_call | solution.py:117
  158.7 3.2 %collective-permute-done.67.chip_ref = f32[15,32,128]{2,1,0:T(8,128)S(1)} collective-permute-done((f32[15,32,128]{2,1,0:T(8,128)S(1)}, f32[15,32,128]{2,1,0:T(8,128)S(1)}, u32[]{:S(2)}, u32[]{:S(2)}) %collective-permute-start.67) | collective-permute-done | bytes 245792 | tf_op jit(solution)/shard_map/ppermute | solution.py:480
  165.6 2.8 %collective-permute-done.70.chip_ref = f32[15,32,128]{2,1,0:T(8,128)S(1)} collective-permute-done((f32[15,32,128]{2,1,0:T(8,128)S(1)}, f32[15,32,128]{2,1,0:T(8,128)S(1)}, u32[]{:S(2)}, u32[]{:S(2)}) %collective-permute-start.70) | collective-permute-done | bytes 245792 | tf_op jit(solution)/shard_map/ppermute | solution.py:480
  172.6 2.5 %shard_map.101 = (f32[16,64,128]{2,1,0:T(8,128)S(1)}, f32[256,128]{1,0:T(8,128)S(1)}, f32[16,64,128]{2,1,0:T(8,128)S(1)}) custom-call(f32[16,32,128]{2,1,0:T(8,128)S(1)} %get-tuple-element.413.low_ref, f32[16,32,128]{2,1,0:T(8,128)S(1)} %get-tuple-element.420.high_ref, f32[16,64,128]{2,1,0:T(8,128)S(1)} %get-tuple-element.421.est_ref, ...), custom_call_target="tpu_custom_call" | custom-call | flops 1000000000 | bytes 3000001 | tf_op jit(solution)/shard_map/pallas_call | solution.py:117
  179.8 3.2 %collective-permute-done.75.chip_ref = f32[15,32,128]{2,1,0:T(8,128)S(1)} collective-permute-done((f32[15,32,128]{2,1,0:T(8,128)S(1)}, f32[15,32,128]{2,1,0:T(8,128)S(1)}, u32[]{:S(2)}, u32[]{:S(2)}) %collective-permute-start.75) | collective-permute-done | bytes 245792 | tf_op jit(solution)/shard_map/ppermute | solution.py:480
  186.7 2.8 %collective-permute-done.77.chip_ref = f32[15,32,128]{2,1,0:T(8,128)S(1)} collective-permute-done((f32[15,32,128]{2,1,0:T(8,128)S(1)}, f32[15,32,128]{2,1,0:T(8,128)S(1)}, u32[]{:S(2)}, u32[]{:S(2)}) %collective-permute-start.77) | collective-permute-done | bytes 245792 | tf_op jit(solution)/shard_map/ppermute | solution.py:480
  198.7 6.5 %collective-permute-done.85.window_ref = f32[4,32,128]{2,1,0:T(8,128)S(1)} collective-permute-done((f32[4,32,128]{2,1,0:T(8,128)S(1)}, f32[4,32,128]{2,1,0:T(8,128)S(1)}, u32[]{:S(2)}, u32[]{:S(2)}) %collective-permute-start.85) | collective-permute-done | bytes 65568 | tf_op jit(solution)/shard_map/ppermute | solution.py:480
  (225 shorter events, 119.6 us)
Async XLA Ops:
  1.3 9.4 %collective-permute-start = (f32[20,32,128]{2,1,0:T(8,128)S(1)}, f32[20,32,128]{2,1,0:T(8,128)S(1)}, u32[]{:S(2)}, u32[]{:S(2)}) collective-permute-start(f32[20,32,128]{2,1,0:T(8,128)S(1)} %get-tuple-element.229), channel_id=1, source_target_pairs={{1,0},{0,2},{2,3},{3,1},{5,4},{4,6},{6,7},{7,5},{9,8},{8,10},{10,1... | collective-permute-start | bytes 983048 | tf_op jit(solution)/shard_map/ppermute | solution.py:480
  1.3 10.9 %collective-permute-start.1 = (f32[20,32,128]{2,1,0:T(8,128)S(1)}, f32[20,32,128]{2,1,0:T(8,128)S(1)}, u32[]{:S(2)}, u32[]{:S(2)}) collective-permute-start(f32[20,32,128]{2,1,0:T(8,128)S(1)} %get-tuple-element.230.kept_ref), channel_id=1, source_target_pairs={{1,2},{2,1},{0,4},{3,7},{5,6},{6,5},{4,0},{7,3},{9,10},{10,9},{8,1... | collective-permute-start | bytes 983048 | tf_op jit(solution)/shard_map/ppermute | solution.py:480
  5.0 14.1 %collective-permute-start.5 = (f32[16,32,128]{2,1,0:T(8,128)S(1)}, f32[16,32,128]{2,1,0:T(8,128)S(1)}, u32[]{:S(2)}, u32[]{:S(2)}) collective-permute-start(f32[16,32,128]{2,1,0:T(8,128)S(1)} %get-tuple-element.458), channel_id=1, source_target_pairs={{1,0},{0,2},{2,3},{3,1},{5,4},{4,6},{6,7},{7,5},{9,8},{8,10},{10,1... | collective-permute-start | bytes 786440 | tf_op jit(solution)/shard_map/ppermute | solution.py:480
  6.9 12.2 %collective-permute-start.6 = (f32[16,32,128]{2,1,0:T(8,128)S(1)}, f32[16,32,128]{2,1,0:T(8,128)S(1)}, u32[]{:S(2)}, u32[]{:S(2)}) collective-permute-start(f32[16,32,128]{2,1,0:T(8,128)S(1)} %get-tuple-element.457.kept_ref), channel_id=1, source_target_pairs={{1,2},{2,1},{0,3},{3,0},{5,6},{6,5},{4,7},{7,4},{9,10},{10,9},{8,1... | collective-permute-start | bytes 786440 | tf_op jit(solution)/shard_map/ppermute | solution.py:480
  14.0 6.0 %collective-permute-start.4 = (f32[15,32,128]{2,1,0:T(8,128)S(1)}, f32[15,32,128]{2,1,0:T(8,128)S(1)}, u32[]{:S(2)}, u32[]{:S(2)}) collective-permute-start(f32[15,32,128]{2,1,0:T(8,128)S(1)} %get-tuple-element.239), channel_id=1, source_target_pairs={{1,4},{4,1},{5,8},{8,5},{9,12},{12,9},{0,2},{13,15},{3,6},{6,3},{7... | collective-permute-start | bytes 737288 | tf_op jit(solution)/shard_map/ppermute | solution.py:480
  15.9 7.4 %collective-permute-start.10 = (f32[15,32,128]{2,1,0:T(8,128)S(1)}, f32[15,32,128]{2,1,0:T(8,128)S(1)}, u32[]{:S(2)}, u32[]{:S(2)}) collective-permute-start(f32[15,32,128]{2,1,0:T(8,128)S(1)} %get-tuple-element.244), channel_id=1, source_target_pairs={{1,4},{4,1},{5,8},{8,5},{9,12},{12,9},{0,2},{13,15},{3,6},{6,3},{7... | collective-permute-start | bytes 737288 | tf_op jit(solution)/shard_map/ppermute | solution.py:480
  23.7 6.5 %collective-permute-start.11 = (f32[15,32,128]{2,1,0:T(8,128)S(1)}, f32[15,32,128]{2,1,0:T(8,128)S(1)}, u32[]{:S(2)}, u32[]{:S(2)}) collective-permute-start(f32[15,32,128]{2,1,0:T(8,128)S(1)} %get-tuple-element.247), channel_id=1, source_target_pairs={{0,1},{1,0},{2,3},{3,2},{4,5},{5,4},{6,7},{7,6},{8,9},{9,8},{10,11... | collective-permute-start | bytes 737288 | tf_op jit(solution)/shard_map/ppermute | solution.py:480
  29.5 7.3 %collective-permute-start.14 = (f32[16,32,128]{2,1,0:T(8,128)S(1)}, f32[16,32,128]{2,1,0:T(8,128)S(1)}, u32[]{:S(2)}, u32[]{:S(2)}) collective-permute-start(f32[16,32,128]{2,1,0:T(8,128)S(1)} %get-tuple-element.258), channel_id=1, source_target_pairs={{1,0},{0,2},{2,3},{3,1},{5,4},{4,6},{6,7},{7,5},{9,8},{8,10},{10,1... | collective-permute-start | bytes 786440 | tf_op jit(solution)/shard_map/ppermute | solution.py:480
  40.1 8.5 %collective-permute-start.20 = (f32[15,32,128]{2,1,0:T(8,128)S(1)}, f32[15,32,128]{2,1,0:T(8,128)S(1)}, u32[]{:S(2)}, u32[]{:S(2)}) collective-permute-start(f32[15,32,128]{2,1,0:T(8,128)S(1)} %get-tuple-element.270), channel_id=1, source_target_pairs={{1,4},{4,1},{5,8},{8,5},{9,12},{12,9},{0,2},{13,15},{3,6},{6,3},{7... | collective-permute-start | bytes 737288 | tf_op jit(solution)/shard_map/ppermute | solution.py:480
  48.9 6.2 %collective-permute-start.21 = (f32[15,32,128]{2,1,0:T(8,128)S(1)}, f32[15,32,128]{2,1,0:T(8,128)S(1)}, u32[]{:S(2)}, u32[]{:S(2)}) collective-permute-start(f32[15,32,128]{2,1,0:T(8,128)S(1)} %get-tuple-element.273), channel_id=1, source_target_pairs={{0,1},{1,0},{2,3},{3,2},{4,5},{5,4},{6,7},{7,6},{8,9},{9,8},{10,11... | collective-permute-start | bytes 737288 | tf_op jit(solution)/shard_map/ppermute | solution.py:480
  49.4 6.2 %collective-permute-start.22 = (f32[15,32,128]{2,1,0:T(8,128)S(1)}, f32[15,32,128]{2,1,0:T(8,128)S(1)}, u32[]{:S(2)}, u32[]{:S(2)}) collective-permute-start(f32[15,32,128]{2,1,0:T(8,128)S(1)} %get-tuple-element.276), channel_id=1, source_target_pairs={{1,4},{4,1},{5,8},{8,5},{9,12},{12,9},{0,2},{13,15},{3,6},{6,3},{7... | collective-permute-start | bytes 737288 | tf_op jit(solution)/shard_map/ppermute | solution.py:480
  53.0 7.0 %collective-permute-start.24 = (f32[16,32,128]{2,1,0:T(8,128)S(1)}, f32[16,32,128]{2,1,0:T(8,128)S(1)}, u32[]{:S(2)}, u32[]{:S(2)}) collective-permute-start(f32[16,32,128]{2,1,0:T(8,128)S(1)} %get-tuple-element.284.kept_ref), channel_id=1, source_target_pairs={{1,2},{2,1},{0,4},{3,7},{5,6},{6,5},{4,0},{7,3},{9,10},{10,9},{8,1... | collective-permute-start | bytes 786440 | tf_op jit(solution)/shard_map/ppermute | solution.py:480
  63.8 8.4 %collective-permute-start.30 = (f32[15,32,128]{2,1,0:T(8,128)S(1)}, f32[15,32,128]{2,1,0:T(8,128)S(1)}, u32[]{:S(2)}, u32[]{:S(2)}) collective-permute-start(f32[15,32,128]{2,1,0:T(8,128)S(1)} %get-tuple-element.300), channel_id=1, source_target_pairs={{1,4},{4,1},{5,8},{8,5},{9,12},{12,9},{0,2},{13,15},{3,6},{6,3},{7... | collective-permute-start | bytes 737288 | tf_op jit(solution)/shard_map/ppermute | solution.py:480
  76.4 6.8 %collective-permute-start.34 = (f32[16,32,128]{2,1,0:T(8,128)S(1)}, f32[16,32,128]{2,1,0:T(8,128)S(1)}, u32[]{:S(2)}, u32[]{:S(2)}) collective-permute-start(f32[16,32,128]{2,1,0:T(8,128)S(1)} %get-tuple-element.314), channel_id=1, source_target_pairs={{1,0},{0,2},{2,3},{3,1},{5,4},{4,6},{6,7},{7,5},{9,8},{8,10},{10,1... | collective-permute-start | bytes 786440 | tf_op jit(solution)/shard_map/ppermute | solution.py:480
  86.3 8.5 %collective-permute-start.40 = (f32[15,32,128]{2,1,0:T(8,128)S(1)}, f32[15,32,128]{2,1,0:T(8,128)S(1)}, u32[]{:S(2)}, u32[]{:S(2)}) collective-permute-start(f32[15,32,128]{2,1,0:T(8,128)S(1)} %get-tuple-element.326), channel_id=1, source_target_pairs={{1,4},{4,1},{5,8},{8,5},{9,12},{12,9},{0,2},{13,15},{3,6},{6,3},{7... | collective-permute-start | bytes 737288 | tf_op jit(solution)/shard_map/ppermute | solution.py:480
  95.2 6.1 %collective-permute-start.41 = (f32[15,32,128]{2,1,0:T(8,128)S(1)}, f32[15,32,128]{2,1,0:T(8,128)S(1)}, u32[]{:S(2)}, u32[]{:S(2)}) collective-permute-start(f32[15,32,128]{2,1,0:T(8,128)S(1)} %get-tuple-element.329), channel_id=1, source_target_pairs={{0,1},{1,0},{2,3},{3,2},{4,5},{5,4},{6,7},{7,6},{8,9},{9,8},{10,11... | collective-permute-start | bytes 737288 | tf_op jit(solution)/shard_map/ppermute | solution.py:480
  95.6 6.2 %collective-permute-start.42 = (f32[15,32,128]{2,1,0:T(8,128)S(1)}, f32[15,32,128]{2,1,0:T(8,128)S(1)}, u32[]{:S(2)}, u32[]{:S(2)}) collective-permute-start(f32[15,32,128]{2,1,0:T(8,128)S(1)} %get-tuple-element.332), channel_id=1, source_target_pairs={{1,4},{4,1},{5,8},{8,5},{9,12},{12,9},{0,2},{13,15},{3,6},{6,3},{7... | collective-permute-start | bytes 737288 | tf_op jit(solution)/shard_map/ppermute | solution.py:480
  99.2 7.0 %collective-permute-start.44 = (f32[16,32,128]{2,1,0:T(8,128)S(1)}, f32[16,32,128]{2,1,0:T(8,128)S(1)}, u32[]{:S(2)}, u32[]{:S(2)}) collective-permute-start(f32[16,32,128]{2,1,0:T(8,128)S(1)} %get-tuple-element.340.kept_ref), channel_id=1, source_target_pairs={{1,2},{2,1},{0,4},{3,7},{5,6},{6,5},{4,0},{7,3},{9,10},{10,9},{8,1... | collective-permute-start | bytes 786440 | tf_op jit(solution)/shard_map/ppermute | solution.py:480
  109.8 5.9 %collective-permute-start.46 = (f32[15,32,128]{2,1,0:T(8,128)S(1)}, f32[15,32,128]{2,1,0:T(8,128)S(1)}, u32[]{:S(2)}, u32[]{:S(2)}) collective-permute-start(f32[15,32,128]{2,1,0:T(8,128)S(1)} %get-tuple-element.349), channel_id=1, source_target_pairs={{1,4},{4,1},{5,8},{8,5},{9,12},{12,9},{0,2},{13,15},{3,6},{6,3},{7... | collective-permute-start | bytes 737288 | tf_op jit(solution)/shard_map/ppermute | solution.py:480
  109.8 8.5 %collective-permute-start.50 = (f32[15,32,128]{2,1,0:T(8,128)S(1)}, f32[15,32,128]{2,1,0:T(8,128)S(1)}, u32[]{:S(2)}, u32[]{:S(2)}) collective-permute-start(f32[15,32,128]{2,1,0:T(8,128)S(1)} %get-tuple-element.356), channel_id=1, source_target_pairs={{1,4},{4,1},{5,8},{8,5},{9,12},{12,9},{0,2},{13,15},{3,6},{6,3},{7... | collective-permute-start | bytes 737288 | tf_op jit(solution)/shard_map/ppermute | solution.py:480
  116.3 5.9 %collective-permute-start.48 = (f32[15,32,128]{2,1,0:T(8,128)S(1)}, f32[15,32,128]{2,1,0:T(8,128)S(1)}, u32[]{:S(2)}, u32[]{:S(2)}) collective-permute-start(f32[15,32,128]{2,1,0:T(8,128)S(1)} %get-tuple-element.354), channel_id=1, source_target_pairs={{1,4},{4,1},{5,8},{8,5},{9,12},{12,9},{0,2},{13,15},{3,6},{6,3},{7... | collective-permute-start | bytes 737288 | tf_op jit(solution)/shard_map/ppermute | solution.py:480
  122.6 6.7 %collective-permute-start.54 = (f32[16,32,128]{2,1,0:T(8,128)S(1)}, f32[16,32,128]{2,1,0:T(8,128)S(1)}, u32[]{:S(2)}, u32[]{:S(2)}) collective-permute-start(f32[16,32,128]{2,1,0:T(8,128)S(1)} %get-tuple-element.370), channel_id=1, source_target_pairs={{1,0},{0,2},{2,3},{3,1},{5,4},{4,6},{6,7},{7,5},{9,8},{8,10},{10,1... | collective-permute-start | bytes 786440 | tf_op jit(solution)/shard_map/ppermute | solution.py:480
  132.3 8.5 %collective-permute-start.60 = (f32[15,32,128]{2,1,0:T(8,128)S(1)}, f32[15,32,128]{2,1,0:T(8,128)S(1)}, u32[]{:S(2)}, u32[]{:S(2)}) collective-permute-start(f32[15,32,128]{2,1,0:T(8,128)S(1)} %get-tuple-element.382), channel_id=1, source_target_pairs={{1,4},{4,1},{5,8},{8,5},{9,12},{12,9},{0,2},{13,15},{3,6},{6,3},{7... | collective-permute-start | bytes 737288 | tf_op jit(solution)/shard_map/ppermute | solution.py:480
  141.2 6.2 %collective-permute-start.61 = (f32[15,32,128]{2,1,0:T(8,128)S(1)}, f32[15,32,128]{2,1,0:T(8,128)S(1)}, u32[]{:S(2)}, u32[]{:S(2)}) collective-permute-start(f32[15,32,128]{2,1,0:T(8,128)S(1)} %get-tuple-element.385), channel_id=1, source_target_pairs={{0,1},{1,0},{2,3},{3,2},{4,5},{5,4},{6,7},{7,6},{8,9},{9,8},{10,11... | collective-permute-start | bytes 737288 | tf_op jit(solution)/shard_map/ppermute | solution.py:480
  141.7 6.2 %collective-permute-start.62 = (f32[15,32,128]{2,1,0:T(8,128)S(1)}, f32[15,32,128]{2,1,0:T(8,128)S(1)}, u32[]{:S(2)}, u32[]{:S(2)}) collective-permute-start(f32[15,32,128]{2,1,0:T(8,128)S(1)} %get-tuple-element.388), channel_id=1, source_target_pairs={{1,4},{4,1},{5,8},{8,5},{9,12},{12,9},{0,2},{13,15},{3,6},{6,3},{7... | collective-permute-start | bytes 737288 | tf_op jit(solution)/shard_map/ppermute | solution.py:480
  145.3 7.0 %collective-permute-start.64 = (f32[16,32,128]{2,1,0:T(8,128)S(1)}, f32[16,32,128]{2,1,0:T(8,128)S(1)}, u32[]{:S(2)}, u32[]{:S(2)}) collective-permute-start(f32[16,32,128]{2,1,0:T(8,128)S(1)} %get-tuple-element.396.kept_ref), channel_id=1, source_target_pairs={{1,2},{2,1},{0,4},{3,7},{5,6},{6,5},{4,0},{7,3},{9,10},{10,9},{8,1... | collective-permute-start | bytes 786440 | tf_op jit(solution)/shard_map/ppermute | solution.py:480
  155.9 8.5 %collective-permute-start.66 = (f32[15,32,128]{2,1,0:T(8,128)S(1)}, f32[15,32,128]{2,1,0:T(8,128)S(1)}, u32[]{:S(2)}, u32[]{:S(2)}) collective-permute-start(f32[15,32,128]{2,1,0:T(8,128)S(1)} %get-tuple-element.403), channel_id=1, source_target_pairs={{1,4},{4,1},{5,8},{8,5},{9,12},{12,9},{0,2},{13,15},{3,6},{6,3},{7... | collective-permute-start | bytes 737288 | tf_op jit(solution)/shard_map/ppermute | solution.py:480
  177.0 8.5 %collective-permute-start.78 = (f32[15,32,128]{2,1,0:T(8,128)S(1)}, f32[15,32,128]{2,1,0:T(8,128)S(1)}, u32[]{:S(2)}, u32[]{:S(2)}) collective-permute-start(f32[15,32,128]{2,1,0:T(8,128)S(1)} %get-tuple-element.435), channel_id=1, source_target_pairs={{1,4},{4,1},{5,8},{8,5},{9,12},{12,9},{0,2},{13,15},{3,6},{6,3},{7... | collective-permute-start | bytes 737288 | tf_op jit(solution)/shard_map/ppermute | solution.py:480
  186.2 5.9 %collective-permute-start.80 = (f32[15,32,128]{2,1,0:T(8,128)S(1)}, f32[15,32,128]{2,1,0:T(8,128)S(1)}, u32[]{:S(2)}, u32[]{:S(2)}) collective-permute-start(f32[15,32,128]{2,1,0:T(8,128)S(1)} %get-tuple-element.440), channel_id=1, source_target_pairs={{1,4},{4,1},{5,8},{8,5},{9,12},{12,9},{0,2},{13,15},{3,6},{6,3},{7... | collective-permute-start | bytes 737288 | tf_op jit(solution)/shard_map/ppermute | solution.py:480
  195.1 10.1 %collective-permute-start.82 = (f32[16,32,128]{2,1,0:T(8,128)S(1)}, f32[16,32,128]{2,1,0:T(8,128)S(1)}, u32[]{:S(2)}, u32[]{:S(2)}) collective-permute-start(f32[16,32,128]{2,1,0:T(8,128)S(1)} %get-tuple-element.445), channel_id=1, source_target_pairs={{0,1},{2,0},{3,2},{1,3},{4,5},{6,4},{7,6},{5,7},{8,9},{10,8},{11,1... | collective-permute-start | bytes 786440 | tf_op jit(solution)/shard_map/ppermute | solution.py:480
  195.6 9.6 %collective-permute-start.83 = (f32[16,32,128]{2,1,0:T(8,128)S(1)}, f32[16,32,128]{2,1,0:T(8,128)S(1)}, u32[]{:S(2)}, u32[]{:S(2)}) collective-permute-start(f32[16,32,128]{2,1,0:T(8,128)S(1)} %get-tuple-element.446.kept_ref), channel_id=1, source_target_pairs={{1,2},{2,1},{0,4},{3,7},{5,6},{6,5},{4,0},{7,3},{9,10},{10,9},{8,1... | collective-permute-start | bytes 786440 | tf_op jit(solution)/shard_map/ppermute | solution.py:480
  198.0 7.2 %collective-permute-start.85 = (f32[4,32,128]{2,1,0:T(8,128)S(1)}, f32[4,32,128]{2,1,0:T(8,128)S(1)}, u32[]{:S(2)}, u32[]{:S(2)}) collective-permute-start(f32[4,32,128]{2,1,0:T(8,128)S(1)} %shard_map.111.window_kept_ref), channel_id=1, source_target_pairs={{1,2},{2,1},{0,4},{3,7},{5,6},{6,5},{4,0},{7,3},{9,10},{10,9},{8,1... | collective-permute-start | bytes 196616 | tf_op jit(solution)/shard_map/ppermute | solution.py:480
  (56 other events, 250.9 us)

commit v2 on v1

--- a/solution.py
+++ b/solution.py
@@ -412,13 +412,16 @@
     lax.fori_loop(0, groups // 2, step, 0)
 
 
-def far_last_kernel(low_ref, high_ref, est_ref, mat_ya, mat_xa, one_out, two_out, corr_out, est):
-    far_kernel(low_ref, high_ref, est_ref, mat_ya, mat_xa, None, None, est, corr_out, None)
-    half = est.shape[1] // 2
+def far_last_kernel(low_ref, high_ref, est_ref, window_ref, mat_ya, mat_xa, one_out, two_out, est, corr):
+    far_kernel(low_ref, high_ref, est_ref, mat_ya, mat_xa, None, None, est, corr, None)
+    planes, rows, cols = est.shape
+    half = rows // 2
     first = place()[1] == 0
-    low, high = est[:, :half], est[:, half:]
-    one_out[...] = jnp.where(first, high, low)
-    two_out[...] = jnp.where(first, low, high)
+    window = (window_ref[...] * corr[...]).reshape(-1, rows, cols)
+    for block, at in ((est[...], slice(0, planes)), (window, slice(planes, None))):
+        low, high = block[:, :half], block[:, half:]
+        one_out[at] = jnp.where(first, high, low)
+        two_out[at] = jnp.where(first, low, high)
 
 
 def near_window(edge_low, edge_high, corr_ref, window_ref, mat_ya, mat_window):
@@ -446,28 +449,22 @@
     put_sent(part_out, (core_ref.at[0], core_ref.at[1]), low_ref, high_ref)
 
 
-def near_last_kernel(edge_low, edge_high, corr_ref, window_ref, mat_ya, mat_window, out_ref):
-    window = near_window(edge_low, edge_high, corr_ref, window_ref, mat_ya, mat_window)
-    each, half, cols = out_ref.shape
-    window = window.reshape(each, 2 * half, cols)
-    out_ref[...] = jnp.where(place()[1] == 0, window[:, :half], window[:, half:])
-
-
-def leave_kernel(one_ref, two_ref, kept_ref, window_ref, window_kept_ref, out_ref):
-    planes, rows, wide = one_ref.shape
+def leave_kernel(one_ref, two_ref, kept_ref, out_ref):
+    planes, rows, cols = out_ref.shape
+    wide = cols // 2
     groups = wide // EDGE
     each = planes // groups
     lower = place()[0] == 0
     one, two = one_ref[...], jnp.where(stays(), kept_ref[...], two_ref[...])
-    window = jnp.where(stays(), window_kept_ref[...], window_ref[...]).reshape(each * rows, wide)
+    window = (one[planes:] + two[planes:]).reshape(each * rows, wide)
     window = jnp.concatenate([window, window], axis=1)
     from_cut = lanes(window.shape, 1) - wide + EDGE // 2
     for g in range(groups):
         at = slice(each * g, each * (g + 1))
         block = jnp.concatenate([jnp.where(lower, two[at], one[at]), jnp.where(lower, one[at], two[at])], axis=2)
-        turned = pltpu.roll(window, (wide - EDGE // 2 - EDGE * g) % (2 * wide), 1)
-        block = jnp.where((from_cut >= 0) & (from_cut < EDGE), turned, block.reshape(each * rows, 2 * wide))
-        out_ref[at] = block.reshape(each, rows, 2 * wide)
+        turned = pltpu.roll(window, (wide - EDGE // 2 - EDGE * g) % cols, 1)
+        block = jnp.where((from_cut >= 0) & (from_cut < EDGE), turned, block.reshape(each * rows, cols))
+        out_ref[at] = block.reshape(each, rows, cols)
 
 
 def local(estimate_start, view_images, psf_taps):
@@ -549,8 +546,11 @@
                 functools.partial(ratio_kernel, side=1), [piece, sent, sent], k_z, own, chip_high, *image
             )
             core_high, chip_high = send(sent_core, core_swap(n)), send(sent_high, chip_swap(n))
-            low, edge_low = call(back_edge_kernel, [piece, edge], k_z, low, chip_low, cost=10)
-            edge_low = send(edge_low, half_swap(n))
+            if last and view + 1 == views:
+                (low,) = call(back_kernel, [piece], k_z, low, chip_low, cost=10)
+            else:
+                low, edge_low = call(back_edge_kernel, [piece, edge], k_z, low, chip_low, cost=10)
+                edge_low = send(edge_low, half_swap(n))
             core_high, _ = lax.optimization_barrier((core_high, low))
             (high,) = call(own_z_half_kernel, [piece], k_z, ratio, core_high)
             if ahead:
@@ -560,19 +560,17 @@
                 else:
                     next_one, next_kept, _ = lax.optimization_barrier((*next_pieces, low))
                     next_one = send(next_one, entry_one(n))
+            if last and view + 1 == views:
+                (high,) = call(back_kernel, [piece], k_z, high, chip_high)
+                one, kept = call(
+                    far_last_kernel, [entry, entry], low, high, main, window, mat_ya, back_x,
+                    scratch=[pltpu.VMEM(field, F32), pltpu.VMEM(packed, F32)],
+                )
+                break
             high, edge_high = call(back_edge_kernel, [piece, edge], k_z, high, chip_high)
             edge_high = send(edge_high, half_swap(n))
             if not ahead:
                 high, edge_low = lax.optimization_barrier((high, edge_low))
-            if last and view + 1 == views:
-                one, kept, corr = call(
-                    far_last_kernel, [piece, piece, packed], low, high, main, mat_ya, back_x,
-                    scratch=[pltpu.VMEM(field, F32)],
-                )
-                (window,) = call(
-                    near_last_kernel, [edge], edge_low, edge_high, corr, window, mat_ya, back_window, cost=10
-                )
-                break
             old_back_x, old_back_window, old_ya = back_x, back_window, mat_ya
             if last:
                 back_x, back_window, mat_x, around, mat_y, mat_ya, k_z = next_mats
@@ -589,8 +587,7 @@
                 edge_low, edge_high, corr, window, part, old_ya, old_back_window, mat_y, around,
             )
     (out,) = call(
-        leave_kernel, [estimate_start.shape],
-        send(one, back(entry_one(n))), send(kept, entry_two(n, True)), kept, send(window, entry_two(n, True)), window,
+        leave_kernel, [estimate_start.shape], send(one, back(entry_one(n))), send(kept, entry_two(n, True)), kept
     )
     return out
 

time: 206 us -> 205 us (level)
  starting transfers between devices: 66.8 us -> 63.2 us
  waiting for transfers between devices: 77.6 us -> 80.7 us
    ppermute x86 -> x83, starting transfers between devices: 66.8 us -> 63.2 us  [local(): send = lambda value, pairs: lax.ppermute(value, AXES, pairs)]
    ppermute x86 -> x83, waiting for transfers between devices: 77.6 us -> 80.7 us  [local(): send = lambda value, pairs: lax.ppermute(value, AXES, pairs)]
    pallas_call x76 -> x75, Pallas kernels: 58.1 us -> 57.5 us  [call(): pl.pallas_call(kernel, out_shape=[jax.ShapeDtypeStruct(s, F32) if isinsta...]
  transfers between devices with their start and end apart: 86 -> 83, of which waited for: 40 -> 41; matrix products, arithmetic and copies ran while one was open for 1% -> 1% of each run, Pallas kernels for 25% -> 24%
where the time goes in v2:
time: 205 us
  waiting for transfers between devices  80.7 us (39%)
  starting transfers between devices  63.2 us (31%)
  Pallas kernels  57.5 us (28%)
  local copies, waits for them, and re-layouts  2.91 us (1%)
    ppermute x83, waiting for transfers between devices, local(): send = lambda value, pairs: lax.ppermute(value, AXES, pairs)  80.7 us
    ppermute x83, starting transfers between devices, local(): send = lambda value, pairs: lax.ppermute(value, AXES, pairs)  63.2 us
    pallas_call x75, Pallas kernels, call(): pl.pallas_call(kernel, out_shape=[jax.ShapeDtypeStruct(s, F32) if isinsta...  57.5 us
  transfers between devices with their start and end apart: 83, of which 41 were waited for; matrix products, arithmetic and copies ran while one was open for 1% of the time, Pallas kernels for 24%

profile of v2, /device:TPU:1, one launch (start us, length us, event | category | flops | bytes accessed | tf_op | source)
XLA Modules:
  0.0 205.0 jit_solution(15370847898490474623)
XLA Ops:
  1.3 2.6 %collective-permute-start.1 = (f32[20,32,128]{2,1,0:T(8,128)S(1)}, f32[20,32,128]{2,1,0:T(8,128)S(1)}, u32[]{:S(2)}, u32[]{:S(2)}) collective-permute-start(f32[20,32,128]{2,1,0:T(8,128)S(1)} %get-tuple-element.223.kept_ref), channel_id=1, source_target_pairs={{1,2},{2,1},{0,4},{3,7},{5,6},{6,5},{4,0},{7,3},{9,10},{10,9},{8,1... | collective-permute-start | bytes 983048 | tf_op jit(solution)/shard_map/ppermute | solution.py:477
  17.0 2.1 %shard_map.40 = (f32[2,16,32,128]{3,2,1,0:T(8,128)S(1)}, bf16[4,2,128,256]{3,2,1,0:T(8,128)(2,1)S(1)}, bf16[2,128,128]{2,1,0:T(8,128)(2,1)S(1)}, bf16[2,128,128]...) custom-call(f32[31,8,128]{2,1,0:T(8,128)S(1)} %get-tuple-element.221, ...), custom_call_target="tpu_custom_call" | custom-call | flops 1 | bytes 1 | tf_op jit(solution)/shard_map/pallas_call | solution.py:117
  20.4 2.9 %collective-permute-start.7 = (f32[15,32,128]{2,1,0:T(8,128)S(1)}, f32[15,32,128]{2,1,0:T(8,128)S(1)}, u32[]{:S(2)}, u32[]{:S(2)}) collective-permute-start(f32[15,32,128]{2,1,0:T(8,128)S(1)} %get-tuple-element.234), channel_id=1, source_target_pairs={{0,1},{1,0},{2,3},{3,2},{4,5},{5,4},{6,7},{7,6},{8,9},{9,8},{10,11... | collective-permute-start | bytes 737288 | tf_op jit(solution)/shard_map/ppermute | solution.py:477
  23.7 2.4 %collective-permute-start.11 = (f32[15,32,128]{2,1,0:T(8,128)S(1)}, f32[15,32,128]{2,1,0:T(8,128)S(1)}, u32[]{:S(2)}, u32[]{:S(2)}) collective-permute-start(f32[15,32,128]{2,1,0:T(8,128)S(1)} %get-tuple-element.240), channel_id=1, source_target_pairs={{0,1},{1,0},{2,3},{3,2},{4,5},{5,4},{6,7},{7,6},{8,9},{9,8},{10,11... | collective-permute-start | bytes 737288 | tf_op jit(solution)/shard_map/ppermute | solution.py:477
  26.6 2.6 %collective-permute-done.8.chip_ref = f32[15,32,128]{2,1,0:T(8,128)S(1)} collective-permute-done((f32[15,32,128]{2,1,0:T(8,128)S(1)}, f32[15,32,128]{2,1,0:T(8,128)S(1)}, u32[]{:S(2)}, u32[]{:S(2)}) %collective-permute-start.8) | collective-permute-done | bytes 245792 | tf_op jit(solution)/shard_map/ppermute | solution.py:477
  34.4 2.5 %shard_map.47 = (f32[16,64,128]{2,1,0:T(8,128)S(1)}, f32[256,128]{1,0:T(8,128)S(1)}, f32[16,64,128]{2,1,0:T(8,128)S(1)}) custom-call(f32[16,32,128]{2,1,0:T(8,128)S(1)} %get-tuple-element.241.low_ref, f32[16,32,128]{2,1,0:T(8,128)S(1)} %get-tuple-element.245.high_ref, f32[16,64,128]{2,1,0:T(8,128)S(1)} %get-tuple-element.246.est_ref, ...), custom_call_target="tpu_custom_call" | custom-call | flops 1000000000 | bytes 3000001 | tf_op jit(solution)/shard_map/pallas_call | solution.py:117
  42.8 3.2 %collective-permute-done.16.chip_ref = f32[15,32,128]{2,1,0:T(8,128)S(1)} collective-permute-done((f32[15,32,128]{2,1,0:T(8,128)S(1)}, f32[15,32,128]{2,1,0:T(8,128)S(1)}, u32[]{:S(2)}, u32[]{:S(2)}) %collective-permute-start.16) | collective-permute-done | bytes 245792 | tf_op jit(solution)/shard_map/ppermute | solution.py:477
  50.3 2.4 %collective-permute-done.18.chip_ref = f32[15,32,128]{2,1,0:T(8,128)S(1)} collective-permute-done((f32[15,32,128]{2,1,0:T(8,128)S(1)}, f32[15,32,128]{2,1,0:T(8,128)S(1)}, u32[]{:S(2)}, u32[]{:S(2)}) %collective-permute-start.18) | collective-permute-done | bytes 245792 | tf_op jit(solution)/shard_map/ppermute | solution.py:477
  53.0 2.1 %collective-permute-start.24 = (f32[16,32,128]{2,1,0:T(8,128)S(1)}, f32[16,32,128]{2,1,0:T(8,128)S(1)}, u32[]{:S(2)}, u32[]{:S(2)}) collective-permute-start(f32[16,32,128]{2,1,0:T(8,128)S(1)} %get-tuple-element.277.kept_ref), channel_id=1, source_target_pairs={{1,2},{2,1},{0,4},{3,7},{5,6},{6,5},{4,0},{7,3},{9,10},{10,9},{8,1... | collective-permute-start | bytes 786440 | tf_op jit(solution)/shard_map/ppermute | solution.py:477
  57.6 2.5 %shard_map.56 = (f32[16,64,128]{2,1,0:T(8,128)S(1)}, f32[256,128]{1,0:T(8,128)S(1)}, f32[16,64,128]{2,1,0:T(8,128)S(1)}) custom-call(f32[16,32,128]{2,1,0:T(8,128)S(1)} %get-tuple-element.267.low_ref, f32[16,32,128]{2,1,0:T(8,128)S(1)} %get-tuple-element.271.high_ref, f32[16,64,128]{2,1,0:T(8,128)S(1)} %get-tuple-element.272.est_ref, ...), custom_call_target="tpu_custom_call" | custom-call | flops 1000000000 | bytes 3000001 | tf_op jit(solution)/shard_map/pallas_call | solution.py:117
  65.4 2.1 %shard_map.58 = (f32[2,16,32,128]{3,2,1,0:T(8,128)S(1)}, bf16[4,2,128,256]{3,2,1,0:T(8,128)(2,1)S(1)}, bf16[2,128,128]{2,1,0:T(8,128)(2,1)S(1)}, bf16[2,128,128]...) custom-call(f32[31,8,128]{2,1,0:T(8,128)S(1)} %get-tuple-element.230, ...), custom_call_target="tpu_custom_call" | custom-call | flops 1 | bytes 1 | tf_op jit(solution)/shard_map/pallas_call | solution.py:117
  67.5 2.1 %collective-permute-done.26.chip_ref = f32[15,32,128]{2,1,0:T(8,128)S(1)} collective-permute-done((f32[15,32,128]{2,1,0:T(8,128)S(1)}, f32[15,32,128]{2,1,0:T(8,128)S(1)}, u32[]{:S(2)}, u32[]{:S(2)}) %collective-permute-start.26) | collective-permute-done | bytes 245792 | tf_op jit(solution)/shard_map/ppermute | solution.py:477
  73.5 2.6 %collective-permute-done.28.chip_ref = f32[15,32,128]{2,1,0:T(8,128)S(1)} collective-permute-done((f32[15,32,128]{2,1,0:T(8,128)S(1)}, f32[15,32,128]{2,1,0:T(8,128)S(1)}, u32[]{:S(2)}, u32[]{:S(2)}) %collective-permute-start.28) | collective-permute-done | bytes 245792 | tf_op jit(solution)/shard_map/ppermute | solution.py:477
  80.8 2.5 %shard_map.65 = (f32[16,64,128]{2,1,0:T(8,128)S(1)}, f32[256,128]{1,0:T(8,128)S(1)}, f32[16,64,128]{2,1,0:T(8,128)S(1)}) custom-call(f32[16,32,128]{2,1,0:T(8,128)S(1)} %get-tuple-element.297.low_ref, f32[16,32,128]{2,1,0:T(8,128)S(1)} %get-tuple-element.301.high_ref, f32[16,64,128]{2,1,0:T(8,128)S(1)} %get-tuple-element.302.est_ref, ...), custom_call_target="tpu_custom_call" | custom-call | flops 1000000000 | bytes 3000001 | tf_op jit(solution)/shard_map/pallas_call | solution.py:117
  89.1 3.2 %collective-permute-done.36.chip_ref = f32[15,32,128]{2,1,0:T(8,128)S(1)} collective-permute-done((f32[15,32,128]{2,1,0:T(8,128)S(1)}, f32[15,32,128]{2,1,0:T(8,128)S(1)}, u32[]{:S(2)}, u32[]{:S(2)}) %collective-permute-start.36) | collective-permute-done | bytes 245792 | tf_op jit(solution)/shard_map/ppermute | solution.py:477
  96.1 2.8 %collective-permute-done.38.chip_ref = f32[15,32,128]{2,1,0:T(8,128)S(1)} collective-permute-done((f32[15,32,128]{2,1,0:T(8,128)S(1)}, f32[15,32,128]{2,1,0:T(8,128)S(1)}, u32[]{:S(2)}, u32[]{:S(2)}) %collective-permute-start.38) | collective-permute-done | bytes 245792 | tf_op jit(solution)/shard_map/ppermute | solution.py:477
  99.2 2.1 %collective-permute-start.44 = (f32[16,32,128]{2,1,0:T(8,128)S(1)}, f32[16,32,128]{2,1,0:T(8,128)S(1)}, u32[]{:S(2)}, u32[]{:S(2)}) collective-permute-start(f32[16,32,128]{2,1,0:T(8,128)S(1)} %get-tuple-element.333.kept_ref), channel_id=1, source_target_pairs={{1,2},{2,1},{0,4},{3,7},{5,6},{6,5},{4,0},{7,3},{9,10},{10,9},{8,1... | collective-permute-start | bytes 786440 | tf_op jit(solution)/shard_map/ppermute | solution.py:477
  103.7 2.5 %shard_map.74 = (f32[16,64,128]{2,1,0:T(8,128)S(1)}, f32[256,128]{1,0:T(8,128)S(1)}, f32[16,64,128]{2,1,0:T(8,128)S(1)}) custom-call(f32[16,32,128]{2,1,0:T(8,128)S(1)} %get-tuple-element.323.low_ref, f32[16,32,128]{2,1,0:T(8,128)S(1)} %get-tuple-element.327.high_ref, f32[16,64,128]{2,1,0:T(8,128)S(1)} %get-tuple-element.328.est_ref, ...), custom_call_target="tpu_custom_call" | custom-call | flops 1000000000 | bytes 3000001 | tf_op jit(solution)/shard_map/pallas_call | solution.py:117
  111.5 2.1 %shard_map.76 = (f32[2,16,32,128]{3,2,1,0:T(8,128)S(1)}, bf16[4,2,128,256]{3,2,1,0:T(8,128)(2,1)S(1)}, bf16[2,128,128]{2,1,0:T(8,128)(2,1)S(1)}, bf16[2,128,128]...) custom-call(f32[31,8,128]{2,1,0:T(8,128)S(1)} %get-tuple-element.284, ...), custom_call_target="tpu_custom_call" | custom-call | flops 1 | bytes 1 | tf_op jit(solution)/shard_map/pallas_call | solution.py:117
  119.5 2.8 %collective-permute-done.48.chip_ref = f32[15,32,128]{2,1,0:T(8,128)S(1)} collective-permute-done((f32[15,32,128]{2,1,0:T(8,128)S(1)}, f32[15,32,128]{2,1,0:T(8,128)S(1)}, u32[]{:S(2)}, u32[]{:S(2)}) %collective-permute-start.48) | collective-permute-done | bytes 245792 | tf_op jit(solution)/shard_map/ppermute | solution.py:477
  126.7 2.5 %shard_map.83 = (f32[16,64,128]{2,1,0:T(8,128)S(1)}, f32[256,128]{1,0:T(8,128)S(1)}, f32[16,64,128]{2,1,0:T(8,128)S(1)}) custom-call(f32[16,32,128]{2,1,0:T(8,128)S(1)} %get-tuple-element.353.low_ref, f32[16,32,128]{2,1,0:T(8,128)S(1)} %get-tuple-element.357.high_ref, f32[16,64,128]{2,1,0:T(8,128)S(1)} %get-tuple-element.358.est_ref, ...), custom_call_target="tpu_custom_call" | custom-call | flops 1000000000 | bytes 3000001 | tf_op jit(solution)/shard_map/pallas_call | solution.py:117
  135.1 3.2 %collective-permute-done.56.chip_ref = f32[15,32,128]{2,1,0:T(8,128)S(1)} collective-permute-done((f32[15,32,128]{2,1,0:T(8,128)S(1)}, f32[15,32,128]{2,1,0:T(8,128)S(1)}, u32[]{:S(2)}, u32[]{:S(2)}) %collective-permute-start.56) | collective-permute-done | bytes 245792 | tf_op jit(solution)/shard_map/ppermute | solution.py:477
  142.2 2.8 %collective-permute-done.58.chip_ref = f32[15,32,128]{2,1,0:T(8,128)S(1)} collective-permute-done((f32[15,32,128]{2,1,0:T(8,128)S(1)}, f32[15,32,128]{2,1,0:T(8,128)S(1)}, u32[]{:S(2)}, u32[]{:S(2)}) %collective-permute-start.58) | collective-permute-done | bytes 245792 | tf_op jit(solution)/shard_map/ppermute | solution.py:477
  145.3 2.1 %collective-permute-start.64 = (f32[16,32,128]{2,1,0:T(8,128)S(1)}, f32[16,32,128]{2,1,0:T(8,128)S(1)}, u32[]{:S(2)}, u32[]{:S(2)}) collective-permute-start(f32[16,32,128]{2,1,0:T(8,128)S(1)} %get-tuple-element.389.kept_ref), channel_id=1, source_target_pairs={{1,2},{2,1},{0,4},{3,7},{5,6},{6,5},{4,0},{7,3},{9,10},{10,9},{8,1... | collective-permute-start | bytes 786440 | tf_op jit(solution)/shard_map/ppermute | solution.py:477
  149.8 2.5 %shard_map.92 = (f32[16,64,128]{2,1,0:T(8,128)S(1)}, f32[256,128]{1,0:T(8,128)S(1)}, f32[16,64,128]{2,1,0:T(8,128)S(1)}) custom-call(f32[16,32,128]{2,1,0:T(8,128)S(1)} %get-tuple-element.379.low_ref, f32[16,32,128]{2,1,0:T(8,128)S(1)} %get-tuple-element.383.high_ref, f32[16,64,128]{2,1,0:T(8,128)S(1)} %get-tuple-element.384.est_ref, ...), custom_call_target="tpu_custom_call" | custom-call | flops 1000000000 | bytes 3000001 | tf_op jit(solution)/shard_map/pallas_call | solution.py:117
  158.7 3.2 %collective-permute-done.67.chip_ref = f32[15,32,128]{2,1,0:T(8,128)S(1)} collective-permute-done((f32[15,32,128]{2,1,0:T(8,128)S(1)}, f32[15,32,128]{2,1,0:T(8,128)S(1)}, u32[]{:S(2)}, u32[]{:S(2)}) %collective-permute-start.67) | collective-permute-done | bytes 245792 | tf_op jit(solution)/shard_map/ppermute | solution.py:477
  165.6 2.8 %collective-permute-done.70.chip_ref = f32[15,32,128]{2,1,0:T(8,128)S(1)} collective-permute-done((f32[15,32,128]{2,1,0:T(8,128)S(1)}, f32[15,32,128]{2,1,0:T(8,128)S(1)}, u32[]{:S(2)}, u32[]{:S(2)}) %collective-permute-start.70) | collective-permute-done | bytes 245792 | tf_op jit(solution)/shard_map/ppermute | solution.py:477
  172.6 2.5 %shard_map.101 = (f32[16,64,128]{2,1,0:T(8,128)S(1)}, f32[256,128]{1,0:T(8,128)S(1)}, f32[16,64,128]{2,1,0:T(8,128)S(1)}) custom-call(f32[16,32,128]{2,1,0:T(8,128)S(1)} %get-tuple-element.406.low_ref, f32[16,32,128]{2,1,0:T(8,128)S(1)} %get-tuple-element.413.high_ref, f32[16,64,128]{2,1,0:T(8,128)S(1)} %get-tuple-element.414.est_ref, ...), custom_call_target="tpu_custom_call" | custom-call | flops 1000000000 | bytes 3000001 | tf_op jit(solution)/shard_map/pallas_call | solution.py:117
  179.8 3.2 %collective-permute-done.75.chip_ref = f32[15,32,128]{2,1,0:T(8,128)S(1)} collective-permute-done((f32[15,32,128]{2,1,0:T(8,128)S(1)}, f32[15,32,128]{2,1,0:T(8,128)S(1)}, u32[]{:S(2)}, u32[]{:S(2)}) %collective-permute-start.75) | collective-permute-done | bytes 245792 | tf_op jit(solution)/shard_map/ppermute | solution.py:477
  186.7 2.8 %collective-permute-done.77.chip_ref = f32[15,32,128]{2,1,0:T(8,128)S(1)} collective-permute-done((f32[15,32,128]{2,1,0:T(8,128)S(1)}, f32[15,32,128]{2,1,0:T(8,128)S(1)}, u32[]{:S(2)}, u32[]{:S(2)}) %collective-permute-start.77) | collective-permute-done | bytes 245792 | tf_op jit(solution)/shard_map/ppermute | solution.py:477
  195.8 3.2 %collective-permute-done.81.one_ref = f32[20,32,128]{2,1,0:T(8,128)S(1)} collective-permute-done((f32[20,32,128]{2,1,0:T(8,128)S(1)}, f32[20,32,128]{2,1,0:T(8,128)S(1)}, u32[]{:S(2)}, u32[]{:S(2)}) %collective-permute-start.81) | collective-permute-done | bytes 327712 | tf_op jit(solution)/shard_map/ppermute | solution.py:477
  199.0 5.1 %collective-permute-done.82.two_ref = f32[20,32,128]{2,1,0:T(8,128)S(1)} collective-permute-done((f32[20,32,128]{2,1,0:T(8,128)S(1)}, f32[20,32,128]{2,1,0:T(8,128)S(1)}, u32[]{:S(2)}, u32[]{:S(2)}) %collective-permute-start.82) | collective-permute-done | bytes 327712 | tf_op jit(solution)/shard_map/ppermute | solution.py:477
  (218 shorter events, 118.8 us)
Async XLA Ops:
  1.3 9.4 %collective-permute-start = (f32[20,32,128]{2,1,0:T(8,128)S(1)}, f32[20,32,128]{2,1,0:T(8,128)S(1)}, u32[]{:S(2)}, u32[]{:S(2)}) collective-permute-start(f32[20,32,128]{2,1,0:T(8,128)S(1)} %get-tuple-element.222), channel_id=1, source_target_pairs={{1,0},{0,2},{2,3},{3,1},{5,4},{4,6},{6,7},{7,5},{9,8},{8,10},{10,1... | collective-permute-start | bytes 983048 | tf_op jit(solution)/shard_map/ppermute | solution.py:477
  1.3 10.9 %collective-permute-start.1 = (f32[20,32,128]{2,1,0:T(8,128)S(1)}, f32[20,32,128]{2,1,0:T(8,128)S(1)}, u32[]{:S(2)}, u32[]{:S(2)}) collective-permute-start(f32[20,32,128]{2,1,0:T(8,128)S(1)} %get-tuple-element.223.kept_ref), channel_id=1, source_target_pairs={{1,2},{2,1},{0,4},{3,7},{5,6},{6,5},{4,0},{7,3},{9,10},{10,9},{8,1... | collective-permute-start | bytes 983048 | tf_op jit(solution)/shard_map/ppermute | solution.py:477
  5.0 14.1 %collective-permute-start.5 = (f32[16,32,128]{2,1,0:T(8,128)S(1)}, f32[16,32,128]{2,1,0:T(8,128)S(1)}, u32[]{:S(2)}, u32[]{:S(2)}) collective-permute-start(f32[16,32,128]{2,1,0:T(8,128)S(1)} %get-tuple-element.444), channel_id=1, source_target_pairs={{1,0},{0,2},{2,3},{3,1},{5,4},{4,6},{6,7},{7,5},{9,8},{8,10},{10,1... | collective-permute-start | bytes 786440 | tf_op jit(solution)/shard_map/ppermute | solution.py:477
  6.9 12.2 %collective-permute-start.6 = (f32[16,32,128]{2,1,0:T(8,128)S(1)}, f32[16,32,128]{2,1,0:T(8,128)S(1)}, u32[]{:S(2)}, u32[]{:S(2)}) collective-permute-start(f32[16,32,128]{2,1,0:T(8,128)S(1)} %get-tuple-element.443.kept_ref), channel_id=1, source_target_pairs={{1,2},{2,1},{0,3},{3,0},{5,6},{6,5},{4,7},{7,4},{9,10},{10,9},{8,1... | collective-permute-start | bytes 786440 | tf_op jit(solution)/shard_map/ppermute | solution.py:477
  14.0 6.0 %collective-permute-start.4 = (f32[15,32,128]{2,1,0:T(8,128)S(1)}, f32[15,32,128]{2,1,0:T(8,128)S(1)}, u32[]{:S(2)}, u32[]{:S(2)}) collective-permute-start(f32[15,32,128]{2,1,0:T(8,128)S(1)} %get-tuple-element.232), channel_id=1, source_target_pairs={{1,4},{4,1},{5,8},{8,5},{9,12},{12,9},{0,2},{13,15},{3,6},{6,3},{7... | collective-permute-start | bytes 737288 | tf_op jit(solution)/shard_map/ppermute | solution.py:477
  15.9 7.4 %collective-permute-start.10 = (f32[15,32,128]{2,1,0:T(8,128)S(1)}, f32[15,32,128]{2,1,0:T(8,128)S(1)}, u32[]{:S(2)}, u32[]{:S(2)}) collective-permute-start(f32[15,32,128]{2,1,0:T(8,128)S(1)} %get-tuple-element.237), channel_id=1, source_target_pairs={{1,4},{4,1},{5,8},{8,5},{9,12},{12,9},{0,2},{13,15},{3,6},{6,3},{7... | collective-permute-start | bytes 737288 | tf_op jit(solution)/shard_map/ppermute | solution.py:477
  23.3 5.9 %collective-permute-start.8 = (f32[15,32,128]{2,1,0:T(8,128)S(1)}, f32[15,32,128]{2,1,0:T(8,128)S(1)}, u32[]{:S(2)}, u32[]{:S(2)}) collective-permute-start(f32[15,32,128]{2,1,0:T(8,128)S(1)} %get-tuple-element.235), channel_id=1, source_target_pairs={{1,4},{4,1},{5,8},{8,5},{9,12},{12,9},{0,2},{13,15},{3,6},{6,3},{7... | collective-permute-start | bytes 737288 | tf_op jit(solution)/shard_map/ppermute | solution.py:477
  23.7 6.5 %collective-permute-start.11 = (f32[15,32,128]{2,1,0:T(8,128)S(1)}, f32[15,32,128]{2,1,0:T(8,128)S(1)}, u32[]{:S(2)}, u32[]{:S(2)}) collective-permute-start(f32[15,32,128]{2,1,0:T(8,128)S(1)} %get-tuple-element.240), channel_id=1, source_target_pairs={{0,1},{1,0},{2,3},{3,2},{4,5},{5,4},{6,7},{7,6},{8,9},{9,8},{10,11... | collective-permute-start | bytes 737288 | tf_op jit(solution)/shard_map/ppermute | solution.py:477
  26.1 5.9 %collective-permute-start.12 = (f32[15,32,128]{2,1,0:T(8,128)S(1)}, f32[15,32,128]{2,1,0:T(8,128)S(1)}, u32[]{:S(2)}, u32[]{:S(2)}) collective-permute-start(f32[15,32,128]{2,1,0:T(8,128)S(1)} %get-tuple-element.243), channel_id=1, source_target_pairs={{1,4},{4,1},{5,8},{8,5},{9,12},{12,9},{0,2},{13,15},{3,6},{6,3},{7... | collective-permute-start | bytes 737288 | tf_op jit(solution)/shard_map/ppermute | solution.py:477
  29.5 7.3 %collective-permute-start.14 = (f32[16,32,128]{2,1,0:T(8,128)S(1)}, f32[16,32,128]{2,1,0:T(8,128)S(1)}, u32[]{:S(2)}, u32[]{:S(2)}) collective-permute-start(f32[16,32,128]{2,1,0:T(8,128)S(1)} %get-tuple-element.251), channel_id=1, source_target_pairs={{1,0},{0,2},{2,3},{3,1},{5,4},{4,6},{6,7},{7,5},{9,8},{8,10},{10,1... | collective-permute-start | bytes 786440 | tf_op jit(solution)/shard_map/ppermute | solution.py:477
  40.1 8.5 %collective-permute-start.20 = (f32[15,32,128]{2,1,0:T(8,128)S(1)}, f32[15,32,128]{2,1,0:T(8,128)S(1)}, u32[]{:S(2)}, u32[]{:S(2)}) collective-permute-start(f32[15,32,128]{2,1,0:T(8,128)S(1)} %get-tuple-element.263), channel_id=1, source_target_pairs={{1,4},{4,1},{5,8},{8,5},{9,12},{12,9},{0,2},{13,15},{3,6},{6,3},{7... | collective-permute-start | bytes 737288 | tf_op jit(solution)/shard_map/ppermute | solution.py:477
  48.9 6.2 %collective-permute-start.21 = (f32[15,32,128]{2,1,0:T(8,128)S(1)}, f32[15,32,128]{2,1,0:T(8,128)S(1)}, u32[]{:S(2)}, u32[]{:S(2)}) collective-permute-start(f32[15,32,128]{2,1,0:T(8,128)S(1)} %get-tuple-element.266), channel_id=1, source_target_pairs={{0,1},{1,0},{2,3},{3,2},{4,5},{5,4},{6,7},{7,6},{8,9},{9,8},{10,11... | collective-permute-start | bytes 737288 | tf_op jit(solution)/shard_map/ppermute | solution.py:477
  49.4 6.2 %collective-permute-start.22 = (f32[15,32,128]{2,1,0:T(8,128)S(1)}, f32[15,32,128]{2,1,0:T(8,128)S(1)}, u32[]{:S(2)}, u32[]{:S(2)}) collective-permute-start(f32[15,32,128]{2,1,0:T(8,128)S(1)} %get-tuple-element.269), channel_id=1, source_target_pairs={{1,4},{4,1},{5,8},{8,5},{9,12},{12,9},{0,2},{13,15},{3,6},{6,3},{7... | collective-permute-start | bytes 737288 | tf_op jit(solution)/shard_map/ppermute | solution.py:477
  53.0 7.0 %collective-permute-start.24 = (f32[16,32,128]{2,1,0:T(8,128)S(1)}, f32[16,32,128]{2,1,0:T(8,128)S(1)}, u32[]{:S(2)}, u32[]{:S(2)}) collective-permute-start(f32[16,32,128]{2,1,0:T(8,128)S(1)} %get-tuple-element.277.kept_ref), channel_id=1, source_target_pairs={{1,2},{2,1},{0,4},{3,7},{5,6},{6,5},{4,0},{7,3},{9,10},{10,9},{8,1... | collective-permute-start | bytes 786440 | tf_op jit(solution)/shard_map/ppermute | solution.py:477
  63.8 8.4 %collective-permute-start.30 = (f32[15,32,128]{2,1,0:T(8,128)S(1)}, f32[15,32,128]{2,1,0:T(8,128)S(1)}, u32[]{:S(2)}, u32[]{:S(2)}) collective-permute-start(f32[15,32,128]{2,1,0:T(8,128)S(1)} %get-tuple-element.293), channel_id=1, source_target_pairs={{1,4},{4,1},{5,8},{8,5},{9,12},{12,9},{0,2},{13,15},{3,6},{6,3},{7... | collective-permute-start | bytes 737288 | tf_op jit(solution)/shard_map/ppermute | solution.py:477
  76.4 6.8 %collective-permute-start.34 = (f32[16,32,128]{2,1,0:T(8,128)S(1)}, f32[16,32,128]{2,1,0:T(8,128)S(1)}, u32[]{:S(2)}, u32[]{:S(2)}) collective-permute-start(f32[16,32,128]{2,1,0:T(8,128)S(1)} %get-tuple-element.307), channel_id=1, source_target_pairs={{1,0},{0,2},{2,3},{3,1},{5,4},{4,6},{6,7},{7,5},{9,8},{8,10},{10,1... | collective-permute-start | bytes 786440 | tf_op jit(solution)/shard_map/ppermute | solution.py:477
  86.3 8.5 %collective-permute-start.40 = (f32[15,32,128]{2,1,0:T(8,128)S(1)}, f32[15,32,128]{2,1,0:T(8,128)S(1)}, u32[]{:S(2)}, u32[]{:S(2)}) collective-permute-start(f32[15,32,128]{2,1,0:T(8,128)S(1)} %get-tuple-element.319), channel_id=1, source_target_pairs={{1,4},{4,1},{5,8},{8,5},{9,12},{12,9},{0,2},{13,15},{3,6},{6,3},{7... | collective-permute-start | bytes 737288 | tf_op jit(solution)/shard_map/ppermute | solution.py:477
  95.2 6.1 %collective-permute-start.41 = (f32[15,32,128]{2,1,0:T(8,128)S(1)}, f32[15,32,128]{2,1,0:T(8,128)S(1)}, u32[]{:S(2)}, u32[]{:S(2)}) collective-permute-start(f32[15,32,128]{2,1,0:T(8,128)S(1)} %get-tuple-element.322), channel_id=1, source_target_pairs={{0,1},{1,0},{2,3},{3,2},{4,5},{5,4},{6,7},{7,6},{8,9},{9,8},{10,11... | collective-permute-start | bytes 737288 | tf_op jit(solution)/shard_map/ppermute | solution.py:477
  95.6 6.2 %collective-permute-start.42 = (f32[15,32,128]{2,1,0:T(8,128)S(1)}, f32[15,32,128]{2,1,0:T(8,128)S(1)}, u32[]{:S(2)}, u32[]{:S(2)}) collective-permute-start(f32[15,32,128]{2,1,0:T(8,128)S(1)} %get-tuple-element.325), channel_id=1, source_target_pairs={{1,4},{4,1},{5,8},{8,5},{9,12},{12,9},{0,2},{13,15},{3,6},{6,3},{7... | collective-permute-start | bytes 737288 | tf_op jit(solution)/shard_map/ppermute | solution.py:477
  99.2 7.0 %collective-permute-start.44 = (f32[16,32,128]{2,1,0:T(8,128)S(1)}, f32[16,32,128]{2,1,0:T(8,128)S(1)}, u32[]{:S(2)}, u32[]{:S(2)}) collective-permute-start(f32[16,32,128]{2,1,0:T(8,128)S(1)} %get-tuple-element.333.kept_ref), channel_id=1, source_target_pairs={{1,2},{2,1},{0,4},{3,7},{5,6},{6,5},{4,0},{7,3},{9,10},{10,9},{8,1... | collective-permute-start | bytes 786440 | tf_op jit(solution)/shard_map/ppermute | solution.py:477
  109.8 8.5 %collective-permute-start.50 = (f32[15,32,128]{2,1,0:T(8,128)S(1)}, f32[15,32,128]{2,1,0:T(8,128)S(1)}, u32[]{:S(2)}, u32[]{:S(2)}) collective-permute-start(f32[15,32,128]{2,1,0:T(8,128)S(1)} %get-tuple-element.349), channel_id=1, source_target_pairs={{1,4},{4,1},{5,8},{8,5},{9,12},{12,9},{0,2},{13,15},{3,6},{6,3},{7... | collective-permute-start | bytes 737288 | tf_op jit(solution)/shard_map/ppermute | solution.py:477
  119.0 5.9 %collective-permute-start.52 = (f32[15,32,128]{2,1,0:T(8,128)S(1)}, f32[15,32,128]{2,1,0:T(8,128)S(1)}, u32[]{:S(2)}, u32[]{:S(2)}) collective-permute-start(f32[15,32,128]{2,1,0:T(8,128)S(1)} %get-tuple-element.355), channel_id=1, source_target_pairs={{1,4},{4,1},{5,8},{8,5},{9,12},{12,9},{0,2},{13,15},{3,6},{6,3},{7... | collective-permute-start | bytes 737288 | tf_op jit(solution)/shard_map/ppermute | solution.py:477
  122.6 6.7 %collective-permute-start.54 = (f32[16,32,128]{2,1,0:T(8,128)S(1)}, f32[16,32,128]{2,1,0:T(8,128)S(1)}, u32[]{:S(2)}, u32[]{:S(2)}) collective-permute-start(f32[16,32,128]{2,1,0:T(8,128)S(1)} %get-tuple-element.363), channel_id=1, source_target_pairs={{1,0},{0,2},{2,3},{3,1},{5,4},{4,6},{6,7},{7,5},{9,8},{8,10},{10,1... | collective-permute-start | bytes 786440 | tf_op jit(solution)/shard_map/ppermute | solution.py:477
  132.3 8.5 %collective-permute-start.60 = (f32[15,32,128]{2,1,0:T(8,128)S(1)}, f32[15,32,128]{2,1,0:T(8,128)S(1)}, u32[]{:S(2)}, u32[]{:S(2)}) collective-permute-start(f32[15,32,128]{2,1,0:T(8,128)S(1)} %get-tuple-element.375), channel_id=1, source_target_pairs={{1,4},{4,1},{5,8},{8,5},{9,12},{12,9},{0,2},{13,15},{3,6},{6,3},{7... | collective-permute-start | bytes 737288 | tf_op jit(solution)/shard_map/ppermute | solution.py:477
  139.1 5.9 %collective-permute-start.58 = (f32[15,32,128]{2,1,0:T(8,128)S(1)}, f32[15,32,128]{2,1,0:T(8,128)S(1)}, u32[]{:S(2)}, u32[]{:S(2)}) collective-permute-start(f32[15,32,128]{2,1,0:T(8,128)S(1)} %get-tuple-element.373), channel_id=1, source_target_pairs={{1,4},{4,1},{5,8},{8,5},{9,12},{12,9},{0,2},{13,15},{3,6},{6,3},{7... | collective-permute-start | bytes 737288 | tf_op jit(solution)/shard_map/ppermute | solution.py:477
  141.2 6.2 %collective-permute-start.61 = (f32[15,32,128]{2,1,0:T(8,128)S(1)}, f32[15,32,128]{2,1,0:T(8,128)S(1)}, u32[]{:S(2)}, u32[]{:S(2)}) collective-permute-start(f32[15,32,128]{2,1,0:T(8,128)S(1)} %get-tuple-element.378), channel_id=1, source_target_pairs={{0,1},{1,0},{2,3},{3,2},{4,5},{5,4},{6,7},{7,6},{8,9},{9,8},{10,11... | collective-permute-start | bytes 737288 | tf_op jit(solution)/shard_map/ppermute | solution.py:477
  141.7 6.2 %collective-permute-start.62 = (f32[15,32,128]{2,1,0:T(8,128)S(1)}, f32[15,32,128]{2,1,0:T(8,128)S(1)}, u32[]{:S(2)}, u32[]{:S(2)}) collective-permute-start(f32[15,32,128]{2,1,0:T(8,128)S(1)} %get-tuple-element.381), channel_id=1, source_target_pairs={{1,4},{4,1},{5,8},{8,5},{9,12},{12,9},{0,2},{13,15},{3,6},{6,3},{7... | collective-permute-start | bytes 737288 | tf_op jit(solution)/shard_map/ppermute | solution.py:477
  145.3 7.0 %collective-permute-start.64 = (f32[16,32,128]{2,1,0:T(8,128)S(1)}, f32[16,32,128]{2,1,0:T(8,128)S(1)}, u32[]{:S(2)}, u32[]{:S(2)}) collective-permute-start(f32[16,32,128]{2,1,0:T(8,128)S(1)} %get-tuple-element.389.kept_ref), channel_id=1, source_target_pairs={{1,2},{2,1},{0,4},{3,7},{5,6},{6,5},{4,0},{7,3},{9,10},{10,9},{8,1... | collective-permute-start | bytes 786440 | tf_op jit(solution)/shard_map/ppermute | solution.py:477
  155.9 8.5 %collective-permute-start.66 = (f32[15,32,128]{2,1,0:T(8,128)S(1)}, f32[15,32,128]{2,1,0:T(8,128)S(1)}, u32[]{:S(2)}, u32[]{:S(2)}) collective-permute-start(f32[15,32,128]{2,1,0:T(8,128)S(1)} %get-tuple-element.396), channel_id=1, source_target_pairs={{1,4},{4,1},{5,8},{8,5},{9,12},{12,9},{0,2},{13,15},{3,6},{6,3},{7... | collective-permute-start | bytes 737288 | tf_op jit(solution)/shard_map/ppermute | solution.py:477
  177.0 8.5 %collective-permute-start.78 = (f32[15,32,128]{2,1,0:T(8,128)S(1)}, f32[15,32,128]{2,1,0:T(8,128)S(1)}, u32[]{:S(2)}, u32[]{:S(2)}) collective-permute-start(f32[15,32,128]{2,1,0:T(8,128)S(1)} %get-tuple-element.427), channel_id=1, source_target_pairs={{1,4},{4,1},{5,8},{8,5},{9,12},{12,9},{0,2},{13,15},{3,6},{6,3},{7... | collective-permute-start | bytes 737288 | tf_op jit(solution)/shard_map/ppermute | solution.py:477
  186.2 5.9 %collective-permute-start.80 = (f32[15,32,128]{2,1,0:T(8,128)S(1)}, f32[15,32,128]{2,1,0:T(8,128)S(1)}, u32[]{:S(2)}, u32[]{:S(2)}) collective-permute-start(f32[15,32,128]{2,1,0:T(8,128)S(1)} %get-tuple-element.432), channel_id=1, source_target_pairs={{1,4},{4,1},{5,8},{8,5},{9,12},{12,9},{0,2},{13,15},{3,6},{6,3},{7... | collective-permute-start | bytes 737288 | tf_op jit(solution)/shard_map/ppermute | solution.py:477
  194.9 9.1 %collective-permute-start.82 = (f32[20,32,128]{2,1,0:T(8,128)S(1)}, f32[20,32,128]{2,1,0:T(8,128)S(1)}, u32[]{:S(2)}, u32[]{:S(2)}) collective-permute-start(f32[20,32,128]{2,1,0:T(8,128)S(1)} %get-tuple-element.436.kept_ref), channel_id=1, source_target_pairs={{1,2},{2,1},{0,4},{3,7},{5,6},{6,5},{4,0},{7,3},{9,10},{10,9},{8,1... | collective-permute-start | bytes 983048 | tf_op jit(solution)/shard_map/ppermute | solution.py:477
  (53 other events, 233.8 us)

commit v3 on v2

--- a/solution.py
+++ b/solution.py
@@ -507,7 +507,7 @@
         functools.partial(mats_kernel, view=0, rows=rows), mats_out, psf_taps, scratch=mats_scratch
     )
     image = pieces(view_images, 0)
-    image = send(image[0], entry_one(n)), send(image[1], entry_two(n, False)), image[1]
+    image = send(image[0], entry_one(n)), send(image[1], entry_two(n, True)), image[1]
     main, window, part, core_low, core_high, *sent_planes = call(
         first_kernel, [field, packed, by_half, sent, sent, sent, sent], one, two, kept, mat_x, around, mat_y
     )

time: 205 us -> 203 us (level)
  waiting for transfers between devices: 80.7 us -> 78.2 us
    ppermute x83, waiting for transfers between devices: 80.7 us -> 78.2 us  [local(): send = lambda value, pairs: lax.ppermute(value, AXES, pairs)]
where the time goes in v3:
time: 203 us; the launch traced here: 202 us
  waiting for transfers between devices  78.2 us (39%)
  starting transfers between devices  63.1 us (31%)
  Pallas kernels  57.4 us (28%)
  local copies, waits for them, and re-layouts  2.91 us (1%)
    ppermute x83, waiting for transfers between devices, local(): send = lambda value, pairs: lax.ppermute(value, AXES, pairs)  78.2 us
    ppermute x83, starting transfers between devices, local(): send = lambda value, pairs: lax.ppermute(value, AXES, pairs)  63.1 us
    pallas_call x75, Pallas kernels, call(): pl.pallas_call(kernel, out_shape=[jax.ShapeDtypeStruct(s, F32) if isinsta...  57.4 us
  transfers between devices with their start and end apart: 83, of which 41 were waited for; matrix products, arithmetic and copies ran while one was open for 1% of the time, Pallas kernels for 24%

profile of v3, /device:TPU:1, one launch (start us, length us, event | category | flops | bytes accessed | tf_op | source)
XLA Modules:
  0.0 202.4 jit_solution(3808220489777615546)
XLA Ops:
  1.3 2.6 %collective-permute-start.1 = (f32[20,32,128]{2,1,0:T(8,128)S(1)}, f32[20,32,128]{2,1,0:T(8,128)S(1)}, u32[]{:S(2)}, u32[]{:S(2)}) collective-permute-start(f32[20,32,128]{2,1,0:T(8,128)S(1)} %get-tuple-element.223.kept_ref), channel_id=1, source_target_pairs={{1,2},{2,1},{0,4},{3,7},{5,6},{6,5},{4,0},{7,3},{9,10},{10,9},{8,1... | collective-permute-start | bytes 983048 | tf_op jit(solution)/shard_map/ppermute | solution.py:477
  17.2 2.1 %shard_map.40 = (f32[2,16,32,128]{3,2,1,0:T(8,128)S(1)}, bf16[4,2,128,256]{3,2,1,0:T(8,128)(2,1)S(1)}, bf16[2,128,128]{2,1,0:T(8,128)(2,1)S(1)}, bf16[2,128,128]...) custom-call(f32[31,8,128]{2,1,0:T(8,128)S(1)} %get-tuple-element.221, ...), custom_call_target="tpu_custom_call" | custom-call | flops 1 | bytes 1 | tf_op jit(solution)/shard_map/pallas_call | solution.py:117
  31.7 2.5 %shard_map.47 = (f32[16,64,128]{2,1,0:T(8,128)S(1)}, f32[256,128]{1,0:T(8,128)S(1)}, f32[16,64,128]{2,1,0:T(8,128)S(1)}) custom-call(f32[16,32,128]{2,1,0:T(8,128)S(1)} %get-tuple-element.241.low_ref, f32[16,32,128]{2,1,0:T(8,128)S(1)} %get-tuple-element.245.high_ref, f32[16,64,128]{2,1,0:T(8,128)S(1)} %get-tuple-element.246.est_ref, ...), custom_call_target="tpu_custom_call" | custom-call | flops 1000000000 | bytes 3000001 | tf_op jit(solution)/shard_map/pallas_call | solution.py:117
  40.2 3.2 %collective-permute-done.16.chip_ref = f32[15,32,128]{2,1,0:T(8,128)S(1)} collective-permute-done((f32[15,32,128]{2,1,0:T(8,128)S(1)}, f32[15,32,128]{2,1,0:T(8,128)S(1)}, u32[]{:S(2)}, u32[]{:S(2)}) %collective-permute-start.16) | collective-permute-done | bytes 245792 | tf_op jit(solution)/shard_map/ppermute | solution.py:477
  48.0 2.0 collective-permute-done.18.chip_ref
  50.4 2.1 %collective-permute-start.24 = (f32[16,32,128]{2,1,0:T(8,128)S(1)}, f32[16,32,128]{2,1,0:T(8,128)S(1)}, u32[]{:S(2)}, u32[]{:S(2)}) collective-permute-start(f32[16,32,128]{2,1,0:T(8,128)S(1)} %get-tuple-element.277.kept_ref), channel_id=1, source_target_pairs={{1,2},{2,1},{0,4},{3,7},{5,6},{6,5},{4,0},{7,3},{9,10},{10,9},{8,1... | collective-permute-start | bytes 786440 | tf_op jit(solution)/shard_map/ppermute | solution.py:477
  54.9 2.5 %shard_map.56 = (f32[16,64,128]{2,1,0:T(8,128)S(1)}, f32[256,128]{1,0:T(8,128)S(1)}, f32[16,64,128]{2,1,0:T(8,128)S(1)}) custom-call(f32[16,32,128]{2,1,0:T(8,128)S(1)} %get-tuple-element.267.low_ref, f32[16,32,128]{2,1,0:T(8,128)S(1)} %get-tuple-element.271.high_ref, f32[16,64,128]{2,1,0:T(8,128)S(1)} %get-tuple-element.272.est_ref, ...), custom_call_target="tpu_custom_call" | custom-call | flops 1000000000 | bytes 3000001 | tf_op jit(solution)/shard_map/pallas_call | solution.py:117
  62.8 2.1 %shard_map.58 = (f32[2,16,32,128]{3,2,1,0:T(8,128)S(1)}, bf16[4,2,128,256]{3,2,1,0:T(8,128)(2,1)S(1)}, bf16[2,128,128]{2,1,0:T(8,128)(2,1)S(1)}, bf16[2,128,128]...) custom-call(f32[31,8,128]{2,1,0:T(8,128)S(1)} %get-tuple-element.230, ...), custom_call_target="tpu_custom_call" | custom-call | flops 1 | bytes 1 | tf_op jit(solution)/shard_map/pallas_call | solution.py:117
  64.9 2.1 %collective-permute-done.26.chip_ref = f32[15,32,128]{2,1,0:T(8,128)S(1)} collective-permute-done((f32[15,32,128]{2,1,0:T(8,128)S(1)}, f32[15,32,128]{2,1,0:T(8,128)S(1)}, u32[]{:S(2)}, u32[]{:S(2)}) %collective-permute-start.26) | collective-permute-done | bytes 245792 | tf_op jit(solution)/shard_map/ppermute | solution.py:477
  71.2 2.3 %collective-permute-done.28.chip_ref = f32[15,32,128]{2,1,0:T(8,128)S(1)} collective-permute-done((f32[15,32,128]{2,1,0:T(8,128)S(1)}, f32[15,32,128]{2,1,0:T(8,128)S(1)}, u32[]{:S(2)}, u32[]{:S(2)}) %collective-permute-start.28) | collective-permute-done | bytes 245792 | tf_op jit(solution)/shard_map/ppermute | solution.py:477
  78.1 2.5 %shard_map.65 = (f32[16,64,128]{2,1,0:T(8,128)S(1)}, f32[256,128]{1,0:T(8,128)S(1)}, f32[16,64,128]{2,1,0:T(8,128)S(1)}) custom-call(f32[16,32,128]{2,1,0:T(8,128)S(1)} %get-tuple-element.297.low_ref, f32[16,32,128]{2,1,0:T(8,128)S(1)} %get-tuple-element.301.high_ref, f32[16,64,128]{2,1,0:T(8,128)S(1)} %get-tuple-element.302.est_ref, ...), custom_call_target="tpu_custom_call" | custom-call | flops 1000000000 | bytes 3000001 | tf_op jit(solution)/shard_map/pallas_call | solution.py:117
  86.4 3.2 %collective-permute-done.36.chip_ref = f32[15,32,128]{2,1,0:T(8,128)S(1)} collective-permute-done((f32[15,32,128]{2,1,0:T(8,128)S(1)}, f32[15,32,128]{2,1,0:T(8,128)S(1)}, u32[]{:S(2)}, u32[]{:S(2)}) %collective-permute-start.36) | collective-permute-done | bytes 245792 | tf_op jit(solution)/shard_map/ppermute | solution.py:477
  93.4 2.8 %collective-permute-done.38.chip_ref = f32[15,32,128]{2,1,0:T(8,128)S(1)} collective-permute-done((f32[15,32,128]{2,1,0:T(8,128)S(1)}, f32[15,32,128]{2,1,0:T(8,128)S(1)}, u32[]{:S(2)}, u32[]{:S(2)}) %collective-permute-start.38) | collective-permute-done | bytes 245792 | tf_op jit(solution)/shard_map/ppermute | solution.py:477
  96.5 2.1 %collective-permute-start.44 = (f32[16,32,128]{2,1,0:T(8,128)S(1)}, f32[16,32,128]{2,1,0:T(8,128)S(1)}, u32[]{:S(2)}, u32[]{:S(2)}) collective-permute-start(f32[16,32,128]{2,1,0:T(8,128)S(1)} %get-tuple-element.333.kept_ref), channel_id=1, source_target_pairs={{1,2},{2,1},{0,4},{3,7},{5,6},{6,5},{4,0},{7,3},{9,10},{10,9},{8,1... | collective-permute-start | bytes 786440 | tf_op jit(solution)/shard_map/ppermute | solution.py:477
  101.1 2.5 %shard_map.74 = (f32[16,64,128]{2,1,0:T(8,128)S(1)}, f32[256,128]{1,0:T(8,128)S(1)}, f32[16,64,128]{2,1,0:T(8,128)S(1)}) custom-call(f32[16,32,128]{2,1,0:T(8,128)S(1)} %get-tuple-element.323.low_ref, f32[16,32,128]{2,1,0:T(8,128)S(1)} %get-tuple-element.327.high_ref, f32[16,64,128]{2,1,0:T(8,128)S(1)} %get-tuple-element.328.est_ref, ...), custom_call_target="tpu_custom_call" | custom-call | flops 1000000000 | bytes 3000001 | tf_op jit(solution)/shard_map/pallas_call | solution.py:117
  108.9 2.1 %shard_map.76 = (f32[2,16,32,128]{3,2,1,0:T(8,128)S(1)}, bf16[4,2,128,256]{3,2,1,0:T(8,128)(2,1)S(1)}, bf16[2,128,128]{2,1,0:T(8,128)(2,1)S(1)}, bf16[2,128,128]...) custom-call(f32[31,8,128]{2,1,0:T(8,128)S(1)} %get-tuple-element.284, ...), custom_call_target="tpu_custom_call" | custom-call | flops 1 | bytes 1 | tf_op jit(solution)/shard_map/pallas_call | solution.py:117
  111.0 2.1 %collective-permute-done.46.chip_ref = f32[15,32,128]{2,1,0:T(8,128)S(1)} collective-permute-done((f32[15,32,128]{2,1,0:T(8,128)S(1)}, f32[15,32,128]{2,1,0:T(8,128)S(1)}, u32[]{:S(2)}, u32[]{:S(2)}) %collective-permute-start.46) | collective-permute-done | bytes 245792 | tf_op jit(solution)/shard_map/ppermute | solution.py:477
  116.8 2.8 %collective-permute-done.48.chip_ref = f32[15,32,128]{2,1,0:T(8,128)S(1)} collective-permute-done((f32[15,32,128]{2,1,0:T(8,128)S(1)}, f32[15,32,128]{2,1,0:T(8,128)S(1)}, u32[]{:S(2)}, u32[]{:S(2)}) %collective-permute-start.48) | collective-permute-done | bytes 245792 | tf_op jit(solution)/shard_map/ppermute | solution.py:477
  124.1 2.5 %shard_map.83 = (f32[16,64,128]{2,1,0:T(8,128)S(1)}, f32[256,128]{1,0:T(8,128)S(1)}, f32[16,64,128]{2,1,0:T(8,128)S(1)}) custom-call(f32[16,32,128]{2,1,0:T(8,128)S(1)} %get-tuple-element.353.low_ref, f32[16,32,128]{2,1,0:T(8,128)S(1)} %get-tuple-element.357.high_ref, f32[16,64,128]{2,1,0:T(8,128)S(1)} %get-tuple-element.358.est_ref, ...), custom_call_target="tpu_custom_call" | custom-call | flops 1000000000 | bytes 3000001 | tf_op jit(solution)/shard_map/pallas_call | solution.py:117
  132.5 3.2 %collective-permute-done.56.chip_ref = f32[15,32,128]{2,1,0:T(8,128)S(1)} collective-permute-done((f32[15,32,128]{2,1,0:T(8,128)S(1)}, f32[15,32,128]{2,1,0:T(8,128)S(1)}, u32[]{:S(2)}, u32[]{:S(2)}) %collective-permute-start.56) | collective-permute-done | bytes 245792 | tf_op jit(solution)/shard_map/ppermute | solution.py:477
  139.6 2.8 %collective-permute-done.58.chip_ref = f32[15,32,128]{2,1,0:T(8,128)S(1)} collective-permute-done((f32[15,32,128]{2,1,0:T(8,128)S(1)}, f32[15,32,128]{2,1,0:T(8,128)S(1)}, u32[]{:S(2)}, u32[]{:S(2)}) %collective-permute-start.58) | collective-permute-done | bytes 245792 | tf_op jit(solution)/shard_map/ppermute | solution.py:477
  142.7 2.1 %collective-permute-start.64 = (f32[16,32,128]{2,1,0:T(8,128)S(1)}, f32[16,32,128]{2,1,0:T(8,128)S(1)}, u32[]{:S(2)}, u32[]{:S(2)}) collective-permute-start(f32[16,32,128]{2,1,0:T(8,128)S(1)} %get-tuple-element.389.kept_ref), channel_id=1, source_target_pairs={{1,2},{2,1},{0,4},{3,7},{5,6},{6,5},{4,0},{7,3},{9,10},{10,9},{8,1... | collective-permute-start | bytes 786440 | tf_op jit(solution)/shard_map/ppermute | solution.py:477
  147.2 2.5 %shard_map.92 = (f32[16,64,128]{2,1,0:T(8,128)S(1)}, f32[256,128]{1,0:T(8,128)S(1)}, f32[16,64,128]{2,1,0:T(8,128)S(1)}) custom-call(f32[16,32,128]{2,1,0:T(8,128)S(1)} %get-tuple-element.379.low_ref, f32[16,32,128]{2,1,0:T(8,128)S(1)} %get-tuple-element.383.high_ref, f32[16,64,128]{2,1,0:T(8,128)S(1)} %get-tuple-element.384.est_ref, ...), custom_call_target="tpu_custom_call" | custom-call | flops 1000000000 | bytes 3000001 | tf_op jit(solution)/shard_map/pallas_call | solution.py:117
  156.0 3.2 %collective-permute-done.67.chip_ref = f32[15,32,128]{2,1,0:T(8,128)S(1)} collective-permute-done((f32[15,32,128]{2,1,0:T(8,128)S(1)}, f32[15,32,128]{2,1,0:T(8,128)S(1)}, u32[]{:S(2)}, u32[]{:S(2)}) %collective-permute-start.67) | collective-permute-done | bytes 245792 | tf_op jit(solution)/shard_map/ppermute | solution.py:477
  159.8 2.0 collective-permute-done.66.chip_ref
  163.0 2.8 %collective-permute-done.70.chip_ref = f32[15,32,128]{2,1,0:T(8,128)S(1)} collective-permute-done((f32[15,32,128]{2,1,0:T(8,128)S(1)}, f32[15,32,128]{2,1,0:T(8,128)S(1)}, u32[]{:S(2)}, u32[]{:S(2)}) %collective-permute-start.70) | collective-permute-done | bytes 245792 | tf_op jit(solution)/shard_map/ppermute | solution.py:477
  169.9 2.5 %shard_map.101 = (f32[16,64,128]{2,1,0:T(8,128)S(1)}, f32[256,128]{1,0:T(8,128)S(1)}, f32[16,64,128]{2,1,0:T(8,128)S(1)}) custom-call(f32[16,32,128]{2,1,0:T(8,128)S(1)} %get-tuple-element.406.low_ref, f32[16,32,128]{2,1,0:T(8,128)S(1)} %get-tuple-element.413.high_ref, f32[16,64,128]{2,1,0:T(8,128)S(1)} %get-tuple-element.414.est_ref, ...), custom_call_target="tpu_custom_call" | custom-call | flops 1000000000 | bytes 3000001 | tf_op jit(solution)/shard_map/pallas_call | solution.py:117
  177.1 3.2 %collective-permute-done.75.chip_ref = f32[15,32,128]{2,1,0:T(8,128)S(1)} collective-permute-done((f32[15,32,128]{2,1,0:T(8,128)S(1)}, f32[15,32,128]{2,1,0:T(8,128)S(1)}, u32[]{:S(2)}, u32[]{:S(2)}) %collective-permute-start.75) | collective-permute-done | bytes 245792 | tf_op jit(solution)/shard_map/ppermute | solution.py:477
  180.9 2.0 collective-permute-done.78.chip_ref
  184.1 2.8 %collective-permute-done.77.chip_ref = f32[15,32,128]{2,1,0:T(8,128)S(1)} collective-permute-done((f32[15,32,128]{2,1,0:T(8,128)S(1)}, f32[15,32,128]{2,1,0:T(8,128)S(1)}, u32[]{:S(2)}, u32[]{:S(2)}) %collective-permute-start.77) | collective-permute-done | bytes 245792 | tf_op jit(solution)/shard_map/ppermute | solution.py:477
  193.2 3.2 %collective-permute-done.81.one_ref = f32[20,32,128]{2,1,0:T(8,128)S(1)} collective-permute-done((f32[20,32,128]{2,1,0:T(8,128)S(1)}, f32[20,32,128]{2,1,0:T(8,128)S(1)}, u32[]{:S(2)}, u32[]{:S(2)}) %collective-permute-start.81) | collective-permute-done | bytes 327712 | tf_op jit(solution)/shard_map/ppermute | solution.py:477
  196.3 5.1 %collective-permute-done.82.two_ref = f32[20,32,128]{2,1,0:T(8,128)S(1)} collective-permute-done((f32[20,32,128]{2,1,0:T(8,128)S(1)}, f32[20,32,128]{2,1,0:T(8,128)S(1)}, u32[]{:S(2)}, u32[]{:S(2)}) %collective-permute-start.82) | collective-permute-done | bytes 327712 | tf_op jit(solution)/shard_map/ppermute | solution.py:477
  (218 shorter events, 118.8 us)
Async XLA Ops:
  1.3 9.4 %collective-permute-start = (f32[20,32,128]{2,1,0:T(8,128)S(1)}, f32[20,32,128]{2,1,0:T(8,128)S(1)}, u32[]{:S(2)}, u32[]{:S(2)}) collective-permute-start(f32[20,32,128]{2,1,0:T(8,128)S(1)} %get-tuple-element.222), channel_id=1, source_target_pairs={{1,0},{0,2},{2,3},{3,1},{5,4},{4,6},{6,7},{7,5},{9,8},{8,10},{10,1... | collective-permute-start | bytes 983048 | tf_op jit(solution)/shard_map/ppermute | solution.py:477
  1.3 11.2 %collective-permute-start.1 = (f32[20,32,128]{2,1,0:T(8,128)S(1)}, f32[20,32,128]{2,1,0:T(8,128)S(1)}, u32[]{:S(2)}, u32[]{:S(2)}) collective-permute-start(f32[20,32,128]{2,1,0:T(8,128)S(1)} %get-tuple-element.223.kept_ref), channel_id=1, source_target_pairs={{1,2},{2,1},{0,4},{3,7},{5,6},{6,5},{4,0},{7,3},{9,10},{10,9},{8,1... | collective-permute-start | bytes 983048 | tf_op jit(solution)/shard_map/ppermute | solution.py:477
  5.0 14.4 %collective-permute-start.5 = (f32[16,32,128]{2,1,0:T(8,128)S(1)}, f32[16,32,128]{2,1,0:T(8,128)S(1)}, u32[]{:S(2)}, u32[]{:S(2)}) collective-permute-start(f32[16,32,128]{2,1,0:T(8,128)S(1)} %get-tuple-element.444), channel_id=1, source_target_pairs={{1,0},{0,2},{2,3},{3,1},{5,4},{4,6},{6,7},{7,5},{9,8},{8,10},{10,1... | collective-permute-start | bytes 786440 | tf_op jit(solution)/shard_map/ppermute | solution.py:477
  6.9 12.5 %collective-permute-start.6 = (f32[16,32,128]{2,1,0:T(8,128)S(1)}, f32[16,32,128]{2,1,0:T(8,128)S(1)}, u32[]{:S(2)}, u32[]{:S(2)}) collective-permute-start(f32[16,32,128]{2,1,0:T(8,128)S(1)} %get-tuple-element.443.kept_ref), channel_id=1, source_target_pairs={{1,2},{2,1},{0,4},{3,7},{5,6},{6,5},{4,0},{7,3},{9,10},{10,9},{8,1... | collective-permute-start | bytes 786440 | tf_op jit(solution)/shard_map/ppermute | solution.py:477
  14.3 6.0 %collective-permute-start.4 = (f32[15,32,128]{2,1,0:T(8,128)S(1)}, f32[15,32,128]{2,1,0:T(8,128)S(1)}, u32[]{:S(2)}, u32[]{:S(2)}) collective-permute-start(f32[15,32,128]{2,1,0:T(8,128)S(1)} %get-tuple-element.232), channel_id=1, source_target_pairs={{1,4},{4,1},{5,8},{8,5},{9,12},{12,9},{0,2},{13,15},{3,6},{6,3},{7... | collective-permute-start | bytes 737288 | tf_op jit(solution)/shard_map/ppermute | solution.py:477
  16.2 6.8 %collective-permute-start.10 = (f32[15,32,128]{2,1,0:T(8,128)S(1)}, f32[15,32,128]{2,1,0:T(8,128)S(1)}, u32[]{:S(2)}, u32[]{:S(2)}) collective-permute-start(f32[15,32,128]{2,1,0:T(8,128)S(1)} %get-tuple-element.237), channel_id=1, source_target_pairs={{1,4},{4,1},{5,8},{8,5},{9,12},{12,9},{0,2},{13,15},{3,6},{6,3},{7... | collective-permute-start | bytes 737288 | tf_op jit(solution)/shard_map/ppermute | solution.py:477
  21.0 6.1 %collective-permute-start.8 = (f32[15,32,128]{2,1,0:T(8,128)S(1)}, f32[15,32,128]{2,1,0:T(8,128)S(1)}, u32[]{:S(2)}, u32[]{:S(2)}) collective-permute-start(f32[15,32,128]{2,1,0:T(8,128)S(1)} %get-tuple-element.235), channel_id=1, source_target_pairs={{1,4},{4,1},{5,8},{8,5},{9,12},{12,9},{0,2},{13,15},{3,6},{6,3},{7... | collective-permute-start | bytes 737288 | tf_op jit(solution)/shard_map/ppermute | solution.py:477
  23.6 6.0 %collective-permute-start.12 = (f32[15,32,128]{2,1,0:T(8,128)S(1)}, f32[15,32,128]{2,1,0:T(8,128)S(1)}, u32[]{:S(2)}, u32[]{:S(2)}) collective-permute-start(f32[15,32,128]{2,1,0:T(8,128)S(1)} %get-tuple-element.243), channel_id=1, source_target_pairs={{1,4},{4,1},{5,8},{8,5},{9,12},{12,9},{0,2},{13,15},{3,6},{6,3},{7... | collective-permute-start | bytes 737288 | tf_op jit(solution)/shard_map/ppermute | solution.py:477
  27.4 6.8 %collective-permute-start.14 = (f32[16,32,128]{2,1,0:T(8,128)S(1)}, f32[16,32,128]{2,1,0:T(8,128)S(1)}, u32[]{:S(2)}, u32[]{:S(2)}) collective-permute-start(f32[16,32,128]{2,1,0:T(8,128)S(1)} %get-tuple-element.251), channel_id=1, source_target_pairs={{1,0},{0,2},{2,3},{3,1},{5,4},{4,6},{6,7},{7,5},{9,8},{8,10},{10,1... | collective-permute-start | bytes 786440 | tf_op jit(solution)/shard_map/ppermute | solution.py:477
  38.5 7.5 %collective-permute-start.20 = (f32[15,32,128]{2,1,0:T(8,128)S(1)}, f32[15,32,128]{2,1,0:T(8,128)S(1)}, u32[]{:S(2)}, u32[]{:S(2)}) collective-permute-start(f32[15,32,128]{2,1,0:T(8,128)S(1)} %get-tuple-element.263), channel_id=1, source_target_pairs={{1,4},{4,1},{5,8},{8,5},{9,12},{12,9},{0,2},{13,15},{3,6},{6,3},{7... | collective-permute-start | bytes 737288 | tf_op jit(solution)/shard_map/ppermute | solution.py:477
  46.3 6.2 %collective-permute-start.21 = (f32[15,32,128]{2,1,0:T(8,128)S(1)}, f32[15,32,128]{2,1,0:T(8,128)S(1)}, u32[]{:S(2)}, u32[]{:S(2)}) collective-permute-start(f32[15,32,128]{2,1,0:T(8,128)S(1)} %get-tuple-element.266), channel_id=1, source_target_pairs={{0,1},{1,0},{2,3},{3,2},{4,5},{5,4},{6,7},{7,6},{8,9},{9,8},{10,11... | collective-permute-start | bytes 737288 | tf_op jit(solution)/shard_map/ppermute | solution.py:477
  46.8 6.2 %collective-permute-start.22 = (f32[15,32,128]{2,1,0:T(8,128)S(1)}, f32[15,32,128]{2,1,0:T(8,128)S(1)}, u32[]{:S(2)}, u32[]{:S(2)}) collective-permute-start(f32[15,32,128]{2,1,0:T(8,128)S(1)} %get-tuple-element.269), channel_id=1, source_target_pairs={{1,4},{4,1},{5,8},{8,5},{9,12},{12,9},{0,2},{13,15},{3,6},{6,3},{7... | collective-permute-start | bytes 737288 | tf_op jit(solution)/shard_map/ppermute | solution.py:477
  50.4 7.0 %collective-permute-start.24 = (f32[16,32,128]{2,1,0:T(8,128)S(1)}, f32[16,32,128]{2,1,0:T(8,128)S(1)}, u32[]{:S(2)}, u32[]{:S(2)}) collective-permute-start(f32[16,32,128]{2,1,0:T(8,128)S(1)} %get-tuple-element.277.kept_ref), channel_id=1, source_target_pairs={{1,2},{2,1},{0,4},{3,7},{5,6},{6,5},{4,0},{7,3},{9,10},{10,9},{8,1... | collective-permute-start | bytes 786440 | tf_op jit(solution)/shard_map/ppermute | solution.py:477
  61.0 5.9 %collective-permute-start.26 = (f32[15,32,128]{2,1,0:T(8,128)S(1)}, f32[15,32,128]{2,1,0:T(8,128)S(1)}, u32[]{:S(2)}, u32[]{:S(2)}) collective-permute-start(f32[15,32,128]{2,1,0:T(8,128)S(1)} %get-tuple-element.286), channel_id=1, source_target_pairs={{1,4},{4,1},{5,8},{8,5},{9,12},{12,9},{0,2},{13,15},{3,6},{6,3},{7... | collective-permute-start | bytes 737288 | tf_op jit(solution)/shard_map/ppermute | solution.py:477
  61.4 8.1 %collective-permute-start.30 = (f32[15,32,128]{2,1,0:T(8,128)S(1)}, f32[15,32,128]{2,1,0:T(8,128)S(1)}, u32[]{:S(2)}, u32[]{:S(2)}) collective-permute-start(f32[15,32,128]{2,1,0:T(8,128)S(1)} %get-tuple-element.293), channel_id=1, source_target_pairs={{1,4},{4,1},{5,8},{8,5},{9,12},{12,9},{0,2},{13,15},{3,6},{6,3},{7... | collective-permute-start | bytes 737288 | tf_op jit(solution)/shard_map/ppermute | solution.py:477
  67.5 5.9 %collective-permute-start.28 = (f32[15,32,128]{2,1,0:T(8,128)S(1)}, f32[15,32,128]{2,1,0:T(8,128)S(1)}, u32[]{:S(2)}, u32[]{:S(2)}) collective-permute-start(f32[15,32,128]{2,1,0:T(8,128)S(1)} %get-tuple-element.291), channel_id=1, source_target_pairs={{1,4},{4,1},{5,8},{8,5},{9,12},{12,9},{0,2},{13,15},{3,6},{6,3},{7... | collective-permute-start | bytes 737288 | tf_op jit(solution)/shard_map/ppermute | solution.py:477
  73.8 6.8 %collective-permute-start.34 = (f32[16,32,128]{2,1,0:T(8,128)S(1)}, f32[16,32,128]{2,1,0:T(8,128)S(1)}, u32[]{:S(2)}, u32[]{:S(2)}) collective-permute-start(f32[16,32,128]{2,1,0:T(8,128)S(1)} %get-tuple-element.307), channel_id=1, source_target_pairs={{1,0},{0,2},{2,3},{3,1},{5,4},{4,6},{6,7},{7,5},{9,8},{8,10},{10,1... | collective-permute-start | bytes 786440 | tf_op jit(solution)/shard_map/ppermute | solution.py:477
  83.7 8.5 %collective-permute-start.40 = (f32[15,32,128]{2,1,0:T(8,128)S(1)}, f32[15,32,128]{2,1,0:T(8,128)S(1)}, u32[]{:S(2)}, u32[]{:S(2)}) collective-permute-start(f32[15,32,128]{2,1,0:T(8,128)S(1)} %get-tuple-element.319), channel_id=1, source_target_pairs={{1,4},{4,1},{5,8},{8,5},{9,12},{12,9},{0,2},{13,15},{3,6},{6,3},{7... | collective-permute-start | bytes 737288 | tf_op jit(solution)/shard_map/ppermute | solution.py:477
  92.5 6.1 %collective-permute-start.41 = (f32[15,32,128]{2,1,0:T(8,128)S(1)}, f32[15,32,128]{2,1,0:T(8,128)S(1)}, u32[]{:S(2)}, u32[]{:S(2)}) collective-permute-start(f32[15,32,128]{2,1,0:T(8,128)S(1)} %get-tuple-element.322), channel_id=1, source_target_pairs={{0,1},{1,0},{2,3},{3,2},{4,5},{5,4},{6,7},{7,6},{8,9},{9,8},{10,11... | collective-permute-start | bytes 737288 | tf_op jit(solution)/shard_map/ppermute | solution.py:477
  92.9 6.2 %collective-permute-start.42 = (f32[15,32,128]{2,1,0:T(8,128)S(1)}, f32[15,32,128]{2,1,0:T(8,128)S(1)}, u32[]{:S(2)}, u32[]{:S(2)}) collective-permute-start(f32[15,32,128]{2,1,0:T(8,128)S(1)} %get-tuple-element.325), channel_id=1, source_target_pairs={{1,4},{4,1},{5,8},{8,5},{9,12},{12,9},{0,2},{13,15},{3,6},{6,3},{7... | collective-permute-start | bytes 737288 | tf_op jit(solution)/shard_map/ppermute | solution.py:477
  96.5 7.0 %collective-permute-start.44 = (f32[16,32,128]{2,1,0:T(8,128)S(1)}, f32[16,32,128]{2,1,0:T(8,128)S(1)}, u32[]{:S(2)}, u32[]{:S(2)}) collective-permute-start(f32[16,32,128]{2,1,0:T(8,128)S(1)} %get-tuple-element.333.kept_ref), channel_id=1, source_target_pairs={{1,2},{2,1},{0,4},{3,7},{5,6},{6,5},{4,0},{7,3},{9,10},{10,9},{8,1... | collective-permute-start | bytes 786440 | tf_op jit(solution)/shard_map/ppermute | solution.py:477
  107.2 8.5 %collective-permute-start.50 = (f32[15,32,128]{2,1,0:T(8,128)S(1)}, f32[15,32,128]{2,1,0:T(8,128)S(1)}, u32[]{:S(2)}, u32[]{:S(2)}) collective-permute-start(f32[15,32,128]{2,1,0:T(8,128)S(1)} %get-tuple-element.349), channel_id=1, source_target_pairs={{1,4},{4,1},{5,8},{8,5},{9,12},{12,9},{0,2},{13,15},{3,6},{6,3},{7... | collective-permute-start | bytes 737288 | tf_op jit(solution)/shard_map/ppermute | solution.py:477
  119.9 6.7 %collective-permute-start.54 = (f32[16,32,128]{2,1,0:T(8,128)S(1)}, f32[16,32,128]{2,1,0:T(8,128)S(1)}, u32[]{:S(2)}, u32[]{:S(2)}) collective-permute-start(f32[16,32,128]{2,1,0:T(8,128)S(1)} %get-tuple-element.363), channel_id=1, source_target_pairs={{1,0},{0,2},{2,3},{3,1},{5,4},{4,6},{6,7},{7,5},{9,8},{8,10},{10,1... | collective-permute-start | bytes 786440 | tf_op jit(solution)/shard_map/ppermute | solution.py:477
  129.7 5.9 %collective-permute-start.56 = (f32[15,32,128]{2,1,0:T(8,128)S(1)}, f32[15,32,128]{2,1,0:T(8,128)S(1)}, u32[]{:S(2)}, u32[]{:S(2)}) collective-permute-start(f32[15,32,128]{2,1,0:T(8,128)S(1)} %get-tuple-element.370), channel_id=1, source_target_pairs={{1,4},{4,1},{5,8},{8,5},{9,12},{12,9},{0,2},{13,15},{3,6},{6,3},{7... | collective-permute-start | bytes 737288 | tf_op jit(solution)/shard_map/ppermute | solution.py:477
  129.7 8.5 %collective-permute-start.60 = (f32[15,32,128]{2,1,0:T(8,128)S(1)}, f32[15,32,128]{2,1,0:T(8,128)S(1)}, u32[]{:S(2)}, u32[]{:S(2)}) collective-permute-start(f32[15,32,128]{2,1,0:T(8,128)S(1)} %get-tuple-element.375), channel_id=1, source_target_pairs={{1,4},{4,1},{5,8},{8,5},{9,12},{12,9},{0,2},{13,15},{3,6},{6,3},{7... | collective-permute-start | bytes 737288 | tf_op jit(solution)/shard_map/ppermute | solution.py:477
  138.6 6.2 %collective-permute-start.61 = (f32[15,32,128]{2,1,0:T(8,128)S(1)}, f32[15,32,128]{2,1,0:T(8,128)S(1)}, u32[]{:S(2)}, u32[]{:S(2)}) collective-permute-start(f32[15,32,128]{2,1,0:T(8,128)S(1)} %get-tuple-element.378), channel_id=1, source_target_pairs={{0,1},{1,0},{2,3},{3,2},{4,5},{5,4},{6,7},{7,6},{8,9},{9,8},{10,11... | collective-permute-start | bytes 737288 | tf_op jit(solution)/shard_map/ppermute | solution.py:477
  139.1 6.2 %collective-permute-start.62 = (f32[15,32,128]{2,1,0:T(8,128)S(1)}, f32[15,32,128]{2,1,0:T(8,128)S(1)}, u32[]{:S(2)}, u32[]{:S(2)}) collective-permute-start(f32[15,32,128]{2,1,0:T(8,128)S(1)} %get-tuple-element.381), channel_id=1, source_target_pairs={{1,4},{4,1},{5,8},{8,5},{9,12},{12,9},{0,2},{13,15},{3,6},{6,3},{7... | collective-permute-start | bytes 737288 | tf_op jit(solution)/shard_map/ppermute | solution.py:477
  142.7 7.0 %collective-permute-start.64 = (f32[16,32,128]{2,1,0:T(8,128)S(1)}, f32[16,32,128]{2,1,0:T(8,128)S(1)}, u32[]{:S(2)}, u32[]{:S(2)}) collective-permute-start(f32[16,32,128]{2,1,0:T(8,128)S(1)} %get-tuple-element.389.kept_ref), channel_id=1, source_target_pairs={{1,2},{2,1},{0,4},{3,7},{5,6},{6,5},{4,0},{7,3},{9,10},{10,9},{8,1... | collective-permute-start | bytes 786440 | tf_op jit(solution)/shard_map/ppermute | solution.py:477
  153.3 8.5 %collective-permute-start.66 = (f32[15,32,128]{2,1,0:T(8,128)S(1)}, f32[15,32,128]{2,1,0:T(8,128)S(1)}, u32[]{:S(2)}, u32[]{:S(2)}) collective-permute-start(f32[15,32,128]{2,1,0:T(8,128)S(1)} %get-tuple-element.396), channel_id=1, source_target_pairs={{1,4},{4,1},{5,8},{8,5},{9,12},{12,9},{0,2},{13,15},{3,6},{6,3},{7... | collective-permute-start | bytes 737288 | tf_op jit(solution)/shard_map/ppermute | solution.py:477
  162.5 5.9 %collective-permute-start.71 = (f32[15,32,128]{2,1,0:T(8,128)S(1)}, f32[15,32,128]{2,1,0:T(8,128)S(1)}, u32[]{:S(2)}, u32[]{:S(2)}) collective-permute-start(f32[15,32,128]{2,1,0:T(8,128)S(1)} %get-tuple-element.408), channel_id=1, source_target_pairs={{1,4},{4,1},{5,8},{8,5},{9,12},{12,9},{0,2},{13,15},{3,6},{6,3},{7... | collective-permute-start | bytes 737288 | tf_op jit(solution)/shard_map/ppermute | solution.py:477
  174.4 8.5 %collective-permute-start.78 = (f32[15,32,128]{2,1,0:T(8,128)S(1)}, f32[15,32,128]{2,1,0:T(8,128)S(1)}, u32[]{:S(2)}, u32[]{:S(2)}) collective-permute-start(f32[15,32,128]{2,1,0:T(8,128)S(1)} %get-tuple-element.427), channel_id=1, source_target_pairs={{1,4},{4,1},{5,8},{8,5},{9,12},{12,9},{0,2},{13,15},{3,6},{6,3},{7... | collective-permute-start | bytes 737288 | tf_op jit(solution)/shard_map/ppermute | solution.py:477
  192.3 9.1 %collective-permute-start.82 = (f32[20,32,128]{2,1,0:T(8,128)S(1)}, f32[20,32,128]{2,1,0:T(8,128)S(1)}, u32[]{:S(2)}, u32[]{:S(2)}) collective-permute-start(f32[20,32,128]{2,1,0:T(8,128)S(1)} %get-tuple-element.436.kept_ref), channel_id=1, source_target_pairs={{1,2},{2,1},{0,4},{3,7},{5,6},{6,5},{4,0},{7,3},{9,10},{10,9},{8,1... | collective-permute-start | bytes 983048 | tf_op jit(solution)/shard_map/ppermute | solution.py:477
  (53 other events, 230.8 us)
